TPU v7x, 32 devices: a whole 2x2x4 slice. The times are simulated.
32 devices in a mesh: ctx: 8 (over z, x), head: 4 (over y, core).
Axes of the slice: x: 2, y: 2, z: 4, core: 2. Of those that a mesh axis runs over, the one named last changes fastest.
Arguments:
- inputs: bfloat16 [8192, 2048], P('ctx', 'head'), may hold values from -6 to 6
- level_factors: float32 [16, 13, 8192], P('head', None, 'ctx'), may hold values from 0.1 to 1
- out_grad: bfloat16 [8192, 2048], P('ctx', 'head'), may hold values from -6 to 6
- master: float32 [3, 2048, 2048], P(None, 'ctx', 'head'), may hold values from -0.125 to 0.125
- moment_one: float32 [3, 2048, 2048], P(None, 'ctx', 'head'), may hold values from -0.024 to 0.024
- moment_two: float32 [3, 2048, 2048], P(None, 'ctx', 'head'), may hold values from 1e-06 to 0.0001
Outputs:
- attention: bfloat16 [8192, 2048], P('ctx', 'head')
- new_weights: bfloat16 [3, 2048, 2048], P(None, None, 'head')
All inputs are finite; a program needn't handle non-finite values.
Results may differ from a plain program's by a relative error of at most 0.0033.
The roundings to bfloat16 on the way count: a program that leaves them out, or rounds other values in their place, can miss the bound.
Values may be sent and summed in bfloat16 or wider, within the bound.
A program may use at most 128 MiB of HBM per device.

v0:
```python
import math

import jax
import jax.numpy as jnp
from jax import lax
from jax.sharding import PartitionSpec as P

LV_IN = 8


PRECISE = lax.Precision.HIGHEST


def from_partner(value, axis, apart):
    mask = 2**apart
    pairs = [(source, source ^ mask) for source in range(lax.axis_size(axis))]
    return lax.ppermute(value, axis, pairs)


def inner_weights(factors_in):
    rows_count = factors_in.shape[2]
    row_pos = lax.broadcasted_iota(jnp.int32, (rows_count, rows_count), 0)
    col_pos = lax.broadcasted_iota(jnp.int32, (rows_count, rows_count), 1)
    crossed = jnp.bitwise_xor(row_pos, col_pos)
    levels = jnp.zeros(crossed.shape, jnp.int32)
    for power in range(factors_in.shape[1] - 1):
        levels = levels + (crossed >= 1 << power).astype(jnp.int32)
    causal = row_pos >= col_pos
    weights = jnp.zeros((factors_in.shape[0], rows_count, rows_count), jnp.float32)
    for level in range(factors_in.shape[1]):
        weights = weights + jnp.where(
            (levels == level)[None], factors_in[:, level, :, None], jnp.float32(0.0)
        )
    return jnp.where(causal[None], weights, jnp.float32(0.0))


def per_head(rows, heads):
    return jnp.transpose(rows.reshape(rows.shape[0], heads, rows.shape[1] // heads), (1, 0, 2))


def body(inputs, level_factors, out_grad, master, moment_one, moment_two):
    tokens_dev = inputs.shape[0]
    heads = level_factors.shape[0]
    head_size = out_grad.shape[1] // heads
    levels_in = LV_IN
    levels_out = level_factors.shape[1] - levels_in
    block_index = lax.axis_index("ctx")
    blocks = lax.axis_size("ctx")
    depth = blocks.bit_length() - 1
    scale = 1.0 / math.sqrt(head_size * tokens_dev)
    whole = lax.all_gather(inputs, "head", axis=1, tiled=True)
    shard_b = master.astype(jnp.bfloat16)
    projected = jnp.einsum(
        "tn,inc->itc",
        whole,
        lax.all_gather(shard_b, "ctx", axis=1, tiled=True),
        preferred_element_type=jnp.float32,
    ).astype(jnp.bfloat16)
    queries_b = per_head(projected[0], heads)
    keys_b = per_head(projected[1], heads)
    values_b = per_head(projected[2], heads)
    grads_b = per_head(out_grad, heads)
    grad_rows = grads_b.astype(jnp.float32)
    own_state = jnp.einsum("htd,hte->hde", keys_b, values_b, preferred_element_type=jnp.float32)
    piece = lax.all_gather(own_state[None], "ctx", axis=0, tiled=True)
    others = lax.broadcasted_iota(jnp.int32, (piece.shape[0],), 0)
    member = []
    for collect_level in range(levels_out):
        upper = block_index >> collect_level & 1 == 1
        same = others >> collect_level + 1 == block_index >> collect_level + 1
        collect_lower = others >> collect_level & 1 == 0
        member.append(jnp.where(upper & same & collect_lower, jnp.float32(1.0), jnp.float32(0.0)))
    member = jnp.stack(member, axis=1)
    buckets = jnp.einsum("nl,nhde->lhde", member, piece, precision=PRECISE)
    buckets_b = buckets.astype(jnp.bfloat16)
    weights = inner_weights(level_factors[:, :levels_in])
    factors_x = level_factors[:, levels_in:]
    factors_lead = jnp.transpose(factors_x, (1, 0, 2))[..., None]
    scores = jnp.einsum("htd,hsd->hts", queries_b, keys_b, preferred_element_type=jnp.float32)
    probs = (scale * scores * weights).astype(jnp.bfloat16)
    inner = jnp.einsum("hts,hsd->htd", probs, values_b, preferred_element_type=jnp.float32)
    reads = jnp.einsum("htd,lhde->lhte", queries_b, buckets_b, preferred_element_type=jnp.float32)
    outer = jnp.sum(factors_lead * reads, axis=0)
    result = (inner + scale * outer).astype(jnp.bfloat16)
    attention = jnp.transpose(result, (1, 0, 2)).reshape(tokens_dev, heads * head_size)
    weighted = (factors_x[:, :, :, None] * grad_rows[:, None]).astype(jnp.bfloat16)
    pending = scale * jnp.einsum(
        "htd,hlte->lhde", queries_b, weighted, preferred_element_type=jnp.float32
    )
    incoming = jnp.zeros((heads, head_size, head_size), jnp.float32)
    for level in range(depth):
        partner = from_partner(pending[level:depth].astype(jnp.bfloat16), "ctx", level).astype(
            jnp.float32
        )
        lower = block_index >> level & 1 == 0
        incoming = incoming + jnp.where(lower, partner[0], jnp.float32(0.0))
        if level + 1 < depth:
            pending = pending.at[level + 1 : depth].add(partner[1:])
    incoming_b = incoming.astype(jnp.bfloat16)
    grad_probs = jnp.einsum("htd,hsd->hts", grads_b, values_b, preferred_element_type=jnp.float32)
    mixed = (scale * grad_probs * weights).astype(jnp.bfloat16)
    backs = jnp.einsum("hte,lhde->lhtd", grads_b, buckets_b, preferred_element_type=jnp.float32)
    grad_q = jnp.einsum(
        "hts,hsd->htd", mixed, keys_b, preferred_element_type=jnp.float32
    ) + scale * jnp.sum(factors_lead * backs, axis=0)
    grad_k = jnp.einsum(
        "hts,htd->hsd", mixed, queries_b, preferred_element_type=jnp.float32
    ) + jnp.einsum("hse,hde->hsd", values_b, incoming_b, preferred_element_type=jnp.float32)
    grad_v = jnp.einsum(
        "hts,htd->hsd", probs, grads_b, preferred_element_type=jnp.float32
    ) + jnp.einsum("hsd,hde->hse", keys_b, incoming_b, preferred_element_type=jnp.float32)
    flat = [
        jnp.transpose(grad_block, (1, 0, 2)).reshape(tokens_dev, heads * head_size)
        for grad_block in (grad_q, grad_k, grad_v)
    ]
    grad_joined = jnp.concatenate(flat, axis=1).astype(jnp.bfloat16)
    owned = lax.psum_scatter(
        jnp.einsum("tr,tc->rc", whole, grad_joined, preferred_element_type=jnp.float32).astype(
            jnp.bfloat16
        ),
        "ctx",
        scatter_dimension=0,
        tiled=True,
    ).astype(jnp.float32)
    owned = owned / (tokens_dev * blocks)
    grad = jnp.transpose(owned.reshape(owned.shape[0], 3, master.shape[2]), (1, 0, 2))
    first = 0.9 * moment_one + 0.1 * grad
    second = 0.95 * moment_two + 0.05 * grad * grad
    updated = master - 0.003 * (first / (jnp.sqrt(second) + 1e-08) + 0.1 * master)
    new_weights = lax.all_gather(updated.astype(jnp.bfloat16), "ctx", axis=1, tiled=True)
    return (attention, new_weights)


def solution(mesh):
    placed = (
        P("ctx", "head"),
        P("head", None, "ctx"),
        P("ctx", "head"),
        P(None, "ctx", "head"),
        P(None, "ctx", "head"),
        P(None, "ctx", "head"),
    )
    return jax.shard_map(
        body,
        mesh=mesh,
        in_specs=placed,
        out_specs=(P("ctx", "head"), P(None, None, "head")),
        check_vma=False,
    )
```

profile of v0, /device:TPU:4, one launch (start us, length us, event | category | flops | bytes accessed | tf_op | source)
XLA Modules:
  0.0 493.2 jit_solution(5162683329529710680)
XLA Ops:
  8.0 2.6 copy.73
  14.3 5.2 %broadcast_compare_fusion = (pred[1024,1024]{1,0:T(8,128)(4,1)}, pred[1024,1024]{1,0:T(8,128)(4,1)}) fusion(), kind=kLoop, calls=%fused_computation.39 | loop fusion | flops 24117248 | bytes 2097152 | tf_op jit(solution)/shard_map/eq | solution.py:32
  19.4 5.1 %broadcast_compare_fusion.2 = (pred[1024,1024]{1,0:T(8,128)(4,1)}, pred[1024,1024]{1,0:T(8,128)(4,1)}) fusion(), kind=kLoop, calls=%fused_computation.41 | loop fusion | flops 24117248 | bytes 2097152 | tf_op jit(solution)/shard_map/eq | solution.py:32
  24.6 5.2 %broadcast_compare_fusion.4 = (pred[1024,1024]{1,0:T(8,128)(4,1)}, pred[1024,1024]{1,0:T(8,128)(4,1)}) fusion(), kind=kLoop, calls=%fused_computation.43 | loop fusion | flops 24117248 | bytes 2097152 | tf_op jit(solution)/shard_map/eq | solution.py:32
  29.7 5.1 %broadcast_compare_fusion.6 = (pred[1024,1024]{1,0:T(8,128)(4,1)}, pred[1024,1024]{1,0:T(8,128)(4,1)}) fusion(), kind=kLoop, calls=%fused_computation.45 | loop fusion | flops 24117248 | bytes 2097152 | tf_op jit(solution)/shard_map/eq | solution.py:32
  34.9 9.3 %all-gather.8.cloned.1.call-done = bf16[1024,2048]{1,0:T(8,128)(2,1)} async-done(((bf16[1024,512]{1,0:T(8,128)(2,1)}), bf16[1024,2048]{1,0:T(8,128)(2,1)}) %all-gather.8.cloned.1.call-update) | async-done | bytes 4194320 | tf_op jit(solution)/shard_map/all_gather | solution.py:51
  44.1 103.8 %all-gather.6.cloned.1.call-done = bf16[3,2048,512]{1,2,0:T(8,128)(2,1)} async-done(((bf16[3,256,512]{1,2,0:T(8,128)(2,1)}), bf16[3,2048,512]{1,2,0:T(8,128)(2,1)}) %all-gather.6.cloned.1.call-update) | async-done | bytes 6291472 | tf_op jit(solution)/shard_map/all_gather | solution.py:56
  147.9 10.2 %convert_bitcast_fusion = bf16[3,1024,512]{1,2,0:T(8,128)(2,1)S(1)} fusion(bf16[3,2048,512]{1,2,0:T(8,128)(2,1)} %all-gather.6.cloned.1.call-done, bf16[1024,2048]{1,0:T(8,128)(2,1)} %all-gather.8.cloned.1.call-done), kind=kOutput, calls=%fused_computation.31 | convolution fusion | flops 6444023808 | bytes 13631488 | tf_op jit(solution)/shard_map/tn,inc->itc/dot_general | solution.py:53
  164.4 3.5 fusion.35
  169.7 21.5 %multiply_convert_fusion = bf16[4,1024,1024]{2,1,0:T(8,128)(2,1)S(1)} fusion(f32[4,1024]{1,0:T(4,128)S(1)} %get-tuple-element.48, f32[4,1024]{1,0:T(4,128)S(1)} %get-tuple-element.42, f32[4,1024]{1,0:T(4,128)S(1)} %get-tuple-element.43, f32[4,1024]{1,0:T(4,128)S(1)} %get-tuple-element.44, f32[4,1024]{1,0:T(4,128)S(1)} %get-tuple-element.45, ...), kind=kOutput, calls=%fused_computation.2 | convolution fusion | flops 1153433600 | bytes 20054016 | tf_op jit(solution)/shard_map/htd,hsd->hts/dot_general | solution.py:79
  191.2 19.4 %fusion = bf16[4,1024,1024]{2,1,0:T(8,128)(2,1)S(1)} fusion(bf16[4,1024,128]{1,2,0:T(8,128)(2,1)S(1)} %bitcast.126, bf16[4,1024,128]{1,2,0:T(8,128)(2,1)S(1)} %bitcast.130, f32[4,1024]{1,0:T(4,128)S(1)} %get-tuple-element.48, f32[4,1024]{1,0:T(4,128)S(1)} %get-tuple-element.42, f32[4,1024]{1,0:T(4,128)S(1)} %get-tuple-element.43, ...), kind=kOutput, calls=%fused_computation.1 | convolution fusion | flops 1153433600 | bytes 20054016 | tf_op jit(solution)/shard_map/htd,hsd->hts/dot_general | solution.py:100
  212.1 6.7 %collective-permute-done.1 = bf16[2,4,128,128]{2,3,0,1:T(8,128)(2,1)S(1)} collective-permute-done((bf16[2,4,128,128]{2,3,0,1:T(8,128)(2,1)S(1)}, bf16[2,4,128,128]{2,3,0,1:T(8,128)(2,1)S(1)}, u32[]{:S(2)}, u32[]{:S(2)}) %collective-permute-start.1) | collective-permute-done | bytes 262176 | tf_op jit(solution)/shard_map/ppermute | solution.py:17
  221.4 5.5 %collective-permute-done.2 = bf16[1,4,128,128]{2,3,0,1:T(8,128)(2,1)S(1)} collective-permute-done((bf16[1,4,128,128]{2,3,0,1:T(8,128)(2,1)S(1)}, bf16[1,4,128,128]{2,3,0,1:T(8,128)(2,1)S(1)}, u32[]{:S(2)}, u32[]{:S(2)}) %collective-permute-start.2) | collective-permute-done | bytes 131104 | tf_op jit(solution)/shard_map/ppermute | solution.py:17
  230.0 4.4 fusion.23
  237.0 6.5 %add_convert_fusion.2 = bf16[4,1024,128]{1,2,0:T(8,128)(2,1)S(1)} fusion(f32[4,1024,128]{1,2,0:T(8,128)S(1)} %fusion.1, bf16[4,1024,1024]{2,1,0:T(8,128)(2,1)} %copy-done.1, bf16[4,1024,128]{1,2,0:T(8,128)(2,1)S(1)} %bitcast.124), kind=kOutput, calls=%fused_computation.37 | convolution fusion | flops 1075314688 | bytes 12582912 | tf_op jit(solution)/shard_map/hts,hsd->htd/dot_general | solution.py:103
  243.5 11.4 %fusion.3 = bf16[2048,1536]{0,1:T(8,128)(2,1)} fusion(bf16[1024,2048]{1,0:T(8,128)(2,1)S(1)} %copy-done.20, bf16[1024,512]{0,1:T(8,128)(2,1)S(1)} %bitcast.139, bf16[1024,512]{0,1:T(8,128)(2,1)S(1)} %bitcast.140, bf16[1024,512]{0,1:T(8,128)(2,1)S(1)} %bitcast.138), kind=kOutput, calls=%fused_computation.10 | convolution fusion | flops 6455033856 | bytes 13631488 | tf_op jit(solution)/shard_map/tr,tc->rc/dot_general | solution.py:118
  255.0 117.2 %reduce-scatter.2.cloned.1.call-done = bf16[256,1536]{0,1:T(8,128)(2,1)} async-done(((bf16[2048,1536]{0,1:T(8,128)(2,1)}), bf16[256,1536]{0,1:T(8,128)(2,1)}) %reduce-scatter.2.cloned.1.call-update) | async-done | bytes 786448 | tf_op jit(solution)/shard_map/reduce_scatter | solution.py:117
  372.2 2.4 convert_multiply_fusion
  374.6 3.1 copy.94
  377.6 4.3 fusion.33
  382.0 3.3 fusion.2
  385.3 6.3 %add_convert_fusion.3 = bf16[4,1024,128]{1,2,0:T(8,128)(2,1)S(1)} fusion(f32[4,1024,128]{1,2,0:T(8,128)S(1)} %fusion.2, bf16[4,1024,1024]{2,1,0:T(8,128)(2,1)} %copy-done, bf16[4,1024,128]{1,2,0:T(8,128)(2,1)S(1)} %bitcast.128), kind=kOutput, calls=%fused_computation.38 | convolution fusion | flops 1075314688 | bytes 12582912 | tf_op jit(solution)/shard_map/hts,hsd->htd/dot_general | solution.py:81
  392.9 87.4 %all-gather.10.cloned.1.call-done = bf16[3,2048,512]{2,1,0:T(8,128)(2,1)} async-done(((bf16[3,256,512]{2,1,0:T(8,128)(2,1)}), bf16[3,2048,512]{2,1,0:T(8,128)(2,1)}) %all-gather.10.cloned.1.call-update) | async-done | bytes 6291472 | tf_op jit(solution)/shard_map/all_gather | solution.py:130
  480.3 5.9 %copy.134 = bf16[3,2048,512]{2,1,0:T(8,128)(2,1)} copy(bf16[3,2048,512]{2,1,0:T(8,128)(2,1)} %all-gather.10.cloned.1.call-done) | data formatting | bytes 12582912
  (84 shorter events, 23.3 us)
Async XLA Ops:
  7.2 37.0 %all-gather.8.cloned.1.call-start = ((), (), s32[]{:S(2)}) async-start(), calls=%async_computation.2 | async-start | bytes 5242880 | tf_op jit(solution)/shard_map/all_gather | solution.py:51
  7.9 140.0 %all-gather.6.cloned.1.call-start = ((), (), s32[]{:S(2)}) async-start(), calls=%async_computation.1 | async-start | bytes 7077888 | tf_op jit(solution)/shard_map/all_gather | solution.py:56
  10.6 219.5 %all-gather.12.cloned.1.call-start = ((), (), s32[]{:S(2)}) async-start(), calls=%async_computation.5 | async-start | bytes 2359296 | tf_op jit(solution)/shard_map/all_gather | solution.py:65
  162.9 209.3 %reduce-scatter.2.cloned.1.call-start = ((), (), s32[]{:S(2)}) async-start(), calls=%async_computation.3 | async-start | bytes 7077888 | tf_op jit(solution)/shard_map/reduce_scatter | solution.py:117
  164.3 5.2 %copy-start.7 = (pred[1024,1024]{1,0:T(8,128)(4,1)S(1)}, pred[1024,1024]{1,0:T(8,128)(4,1)}, u32[]{:S(2)}) copy-start(pred[1024,1024]{1,0:T(8,128)(4,1)} %iota_compare_fusion) | copy-start | bytes 3145732
  164.3 5.2 %copy-start.8 = (pred[1024,1024]{1,0:T(8,128)(4,1)S(1)}, pred[1024,1024]{1,0:T(8,128)(4,1)}, u32[]{:S(2)}) copy-start(pred[1024,1024]{1,0:T(8,128)(4,1)} %get-tuple-element.53) | copy-start | bytes 3145732
  164.3 5.2 %copy-start.9 = (pred[1024,1024]{1,0:T(8,128)(4,1)S(1)}, pred[1024,1024]{1,0:T(8,128)(4,1)}, u32[]{:S(2)}) copy-start(pred[1024,1024]{1,0:T(8,128)(4,1)} %get-tuple-element.54) | copy-start | bytes 3145732
  164.3 5.2 %copy-start.10 = (pred[1024,1024]{1,0:T(8,128)(4,1)S(1)}, pred[1024,1024]{1,0:T(8,128)(4,1)}, u32[]{:S(2)}) copy-start(pred[1024,1024]{1,0:T(8,128)(4,1)} %get-tuple-element.55) | copy-start | bytes 3145732
  164.3 5.2 %copy-start.11 = (pred[1024,1024]{1,0:T(8,128)(4,1)S(1)}, pred[1024,1024]{1,0:T(8,128)(4,1)}, u32[]{:S(2)}) copy-start(pred[1024,1024]{1,0:T(8,128)(4,1)} %get-tuple-element.56) | copy-start | bytes 3145732
  164.3 5.2 %copy-start.12 = (pred[1024,1024]{1,0:T(8,128)(4,1)S(1)}, pred[1024,1024]{1,0:T(8,128)(4,1)}, u32[]{:S(2)}) copy-start(pred[1024,1024]{1,0:T(8,128)(4,1)} %get-tuple-element.57) | copy-start | bytes 3145732
  164.3 5.2 %copy-start.13 = (pred[1024,1024]{1,0:T(8,128)(4,1)S(1)}, pred[1024,1024]{1,0:T(8,128)(4,1)}, u32[]{:S(2)}) copy-start(pred[1024,1024]{1,0:T(8,128)(4,1)} %get-tuple-element.58) | copy-start | bytes 3145732
  164.3 5.2 %copy-start.14 = (pred[1024,1024]{1,0:T(8,128)(4,1)S(1)}, pred[1024,1024]{1,0:T(8,128)(4,1)}, u32[]{:S(2)}) copy-start(pred[1024,1024]{1,0:T(8,128)(4,1)} %get-tuple-element.59) | copy-start | bytes 3145732
  164.4 5.3 %copy-start.15 = (pred[1024,1024]{1,0:T(8,128)(4,1)S(1)}, pred[1024,1024]{1,0:T(8,128)(4,1)}, u32[]{:S(2)}) copy-start(pred[1024,1024]{1,0:T(8,128)(4,1)} %get-tuple-element.60) | copy-start | bytes 3145732
  168.0 42.6 %collective-permute-start = (bf16[3,4,128,128]{2,3,0,1:T(8,128)(2,1)S(1)}, bf16[3,4,128,128]{2,3,0,1:T(8,128)(2,1)S(1)}, u32[]{:S(2)}, u32[]{:S(2)}) collective-permute-start(bf16[3,4,128,128]{2,3,0,1:T(8,128)(2,1)S(1)} %slice.181), channel_id=1, source_target_pairs={{0,4},{4,0},{8,12},{12,8},{16,20},{20,16},{24,28},{28,24},{1,5},{5... | collective-permute-start | bytes 1179656 | tf_op jit(solution)/shard_map/ppermute | solution.py:17
  191.2 19.7 %copy-start = (bf16[4,1024,1024]{2,1,0:T(8,128)(2,1)}, bf16[4,1024,1024]{2,1,0:T(8,128)(2,1)S(1)}, u32[]{:S(2)}) copy-start(bf16[4,1024,1024]{2,1,0:T(8,128)(2,1)S(1)} %multiply_convert_fusion) | copy-start | bytes 25165828
  210.6 9.5 %copy-start.1 = (bf16[4,1024,1024]{2,1,0:T(8,128)(2,1)}, bf16[4,1024,1024]{2,1,0:T(8,128)(2,1)S(1)}, u32[]{:S(2)}) copy-start(bf16[4,1024,1024]{2,1,0:T(8,128)(2,1)S(1)} %fusion) | copy-start | bytes 25165828
  210.8 9.4 %copy-start.2 = (bf16[1,1024,512]{1,2,0:T(8,128)(2,1)S(1)}, bf16[1,1024,512]{1,2,0:T(8,128)(2,1)}, u32[]{:S(2)}) copy-start(bf16[1,1024,512]{1,2,0:T(8,128)(2,1)} %get-tuple-element.38) | copy-start | bytes 3145732
  210.8 8.0 %collective-permute-start.1 = (bf16[2,4,128,128]{2,3,0,1:T(8,128)(2,1)S(1)}, bf16[2,4,128,128]{2,3,0,1:T(8,128)(2,1)S(1)}, u32[]{:S(2)}, u32[]{:S(2)}) collective-permute-start(bf16[2,4,128,128]{2,3,0,1:T(8,128)(2,1)S(1)} %get-tuple-element.34), channel_id=1, source_target_pairs={{0,8},{4,12},{8,0},{12,4},{16,24},{20,28},{24,16},{28,20},{1,9},{5... | collective-permute-start | bytes 786440 | tf_op jit(solution)/shard_map/ppermute | solution.py:17
  218.9 8.1 %collective-permute-start.2 = (bf16[1,4,128,128]{2,3,0,1:T(8,128)(2,1)S(1)}, bf16[1,4,128,128]{2,3,0,1:T(8,128)(2,1)S(1)}, u32[]{:S(2)}, u32[]{:S(2)}) collective-permute-start(bf16[1,4,128,128]{2,3,0,1:T(8,128)(2,1)S(1)} %fusion.43), channel_id=1, source_target_pairs={{0,16},{4,20},{8,24},{12,28},{16,0},{20,4},{24,8},{28,12},{1,17},{... | collective-permute-start | bytes 393224 | tf_op jit(solution)/shard_map/ppermute | solution.py:17
  237.0 6.5 %copy-start.17 = (bf16[4,1024,128]{1,2,0:T(8,128)(2,1)S(1)}, bf16[4,1024,128]{1,2,0:T(8,128)(2,1)}, u32[]{:S(2)}) copy-start(bf16[4,1024,128]{1,2,0:T(8,128)(2,1)} %add_convert_fusion) | copy-start | bytes 3145732
  237.0 6.5 %copy-start.18 = (bf16[4,1024,128]{1,2,0:T(8,128)(2,1)S(1)}, bf16[4,1024,128]{1,2,0:T(8,128)(2,1)}, u32[]{:S(2)}) copy-start(bf16[4,1024,128]{1,2,0:T(8,128)(2,1)} %add_convert_fusion.1) | copy-start | bytes 3145732
  237.0 6.5 %copy-start.20 = (bf16[1024,2048]{1,0:T(8,128)(2,1)S(1)}, bf16[1024,2048]{1,0:T(8,128)(2,1)}, u32[]{:S(2)}) copy-start(bf16[1024,2048]{1,0:T(8,128)(2,1)} %all-gather.8.cloned.1.call-done) | copy-start | bytes 12582916
  255.0 122.7 %copy-start.3 = (f32[3,256,512]{2,1,0:T(8,128)S(1)}, f32[3,256,512]{2,1,0:T(8,128)}, u32[]{:S(2)}) copy-start(f32[3,256,512]{2,1,0:T(8,128)} %param.13) | copy-start | bytes 4718596
  255.0 225.4 %all-gather.10.cloned.1.call-start = ((), (), s32[]{:S(2)}) async-start(), calls=%async_computation.4 | async-start | bytes 7077888 | tf_op jit(solution)/shard_map/all_gather | solution.py:130
  (5 other events, 18.4 us)
Sparse Core Ops, SparseCore 0:
  9.6 34.5 all-gather.7
  46.8 101.0 all-gather.5
  163.0 50.0 all-gather.11
  255.1 117.0 reduce-scatter.1
  382.1 98.1 all-gather.9
where the time goes:
time: 502 us; the launch traced here: 493 us
  waiting for transfers between devices  331 us (66%)
  matrix products  94.9 us (19%)
  other arithmetic  30.4 us (6%)
  local copies, waits for them, and re-layouts  19.6 us (4%)
  between operations  14.7 us (3%)
    reduce_scatter x1, waiting for transfers between devices, body(): lax.psum_scatter(jnp.einsum('tr,tc->rc', whole, grad_joined, preferred_el...  117 us
    all_gather x1, waiting for transfers between devices, body(): lax.all_gather(shard_b, 'ctx', axis=1, tiled=True)  104 us
    all_gather x1, waiting for transfers between devices, body(): lax.all_gather(updated.astype(jnp.bfloat16), 'ctx', axis=1, tiled=True)  87.4 us
    dot_general x1, matrix products, body(): jnp.einsum('htd,hsd->hts', queries_b, keys_b, preferred_element_type=jnp....  21.5 us
    eq x4, other arithmetic, inner_weights(): levels == level  20.6 us
    dot_general x1, matrix products, body(): jnp.einsum('htd,hsd->hts', grads_b, values_b, preferred_element_type=jnp....  19.4 us
    ppermute x3, waiting for transfers between devices, from_partner(): return lax.ppermute(value, axis, pairs)  12.2 us
    dot_general x1, matrix products, body(): jnp.einsum('tr,tc->rc', whole, grad_joined, preferred_element_type=jnp.fl...  11.4 us
  transfers between devices with their start and end apart: 8, of which 6 were waited for; matrix products, arithmetic and copies ran while one was open for 18% of the time, Pallas kernels for 0%

commit v1 on v0

v1 whole, which is shorter than its diff:
```python
import functools
import math

import jax
import jax.numpy as jnp
from jax import lax
from jax.experimental import pallas as pl
from jax.experimental.pallas import tpu as pltpu
from jax.sharding import PartitionSpec as P

LV_IN = 8
MESH = pl.DeviceIdType.MESH
F32 = jnp.float32
BF16 = jnp.bfloat16
VMEM_LIMIT = 56 * 1024 * 1024


def factor_ctx(count):
    nx = 1 << ((count.bit_length() - 1) // 2)
    return count // nx, nx


class Gather:
    def __init__(self, ref, nz, nx, rows, sz, rz, sx, rx):
        self.ref, self.nz, self.nx, self.rows = ref, nz, nx, rows
        self.sz, self.rz, self.sx, self.rx = sz, rz, sx, rx
        me = lax.axis_index("ctx")
        self.z, self.x = me // nx, me % nx
        self.started = []

    def piece(self, i, d, z, x):
        half = self.rows // 2
        start = pl.multiple_of((z * self.nx + x) * self.rows + d * half, half)
        return self.ref.at[i, pl.ds(start, half), :]

    def origin(self, d, t):
        return (self.z + (self.nz - t if d == 0 else t)) % self.nz

    def ring_peer(self, d):
        return ((self.z + (1 if d == 0 else self.nz - 1)) % self.nz) * self.nx + self.x

    def ring_copy(self, i, d, s, z):
        view = self.piece(i, d, z, self.x)
        return pltpu.make_async_remote_copy(
            src_ref=view, dst_ref=view, send_sem=self.sz.at[i, d, s], recv_sem=self.rz.at[i, d, s],
            device_id={"ctx": self.ring_peer(d)}, device_id_type=MESH)

    def side_copy(self, i, d, t, p, x):
        view = self.piece(i, d, self.origin(d, t), x)
        return pltpu.make_async_remote_copy(
            src_ref=view, dst_ref=view, send_sem=self.sx.at[i, d, t, p - 1], recv_sem=self.rx.at[i, d, t, p - 1],
            device_id={"ctx": self.z * self.nx + (self.x + p) % self.nx}, device_id_type=MESH)

    def send(self, i, d, t):
        if t < self.nz - 1:
            copy = self.ring_copy(i, d, t, self.origin(d, t))
            copy.start()
            self.started.append(copy)
        for p in range(1, self.nx):
            copy = self.side_copy(i, d, t, p, self.x)
            copy.start()
            self.started.append(copy)

    def ring_step(self, i, d, s):
        self.ring_copy(i, d, s, self.origin(d, s + 1)).wait_recv()
        self.send(i, d, s + 1)

    def wait_side(self, i):
        for t in range(self.nz):
            for d in range(2):
                for p in range(1, self.nx):
                    self.side_copy(i, d, t, p, (self.x + self.nx - p) % self.nx).wait_recv()

    def finish(self):
        for copy in self.started:
            copy.wait_send()


def ctx_peers(nz, nx):
    me = lax.axis_index("ctx")
    z, x = me // nx, me % nx
    peers = [{"ctx": ((z + 1) % nz) * nx + x}, {"ctx": ((z + nz - 1) % nz) * nx + x}]
    peers += [{"ctx": z * nx + (x + p) % nx} for p in range(1, nx)]
    return peers


def greet(peers):
    barrier = pltpu.get_barrier_semaphore()
    for peer in peers:
        pl.semaphore_signal(barrier, inc=1, device_id=peer, device_id_type=MESH)
    pl.semaphore_wait(barrier, len(peers))


def project_kernel(nz, nx, nh, x_ref, m_ref, p_ref, xt_ref, xs, ws, sz, rz, sx, rx, sy, ry, sc, rc):
    rows = m_ref.shape[1]
    width = x_ref.shape[1]
    ny = nh // 2
    head = lax.axis_index("head")
    y, core = head // 2, head % 2
    sibling = {"head": y * 2 + 1 - core}
    peers = ctx_peers(nz, nx) + [sibling]
    peers += [{"head": ((y + p) % ny) * 2 + core} for p in range(1, ny)]
    gather = Gather(ws, nz, nx, rows, sz, rz, sx, rx)
    own = pl.multiple_of(lax.axis_index("ctx") * rows, rows)
    for i in range(3):
        ws[i, pl.ds(own, rows), :] = m_ref[i].astype(BF16)

    def columns(h):
        return xs.at[:, pl.ds(pl.multiple_of(h * width, width), width)]

    greet(peers)
    xs[:, pl.ds(pl.multiple_of(head * width, width), width)] = x_ref[...]
    started = []

    def y_copy(p, h):
        return pltpu.make_async_remote_copy(
            src_ref=columns(h), dst_ref=columns(h), send_sem=sy.at[p], recv_sem=ry.at[p],
            device_id={"head": ((y + p) % ny) * 2 + core}, device_id_type=MESH)

    def core_copy(p, h):
        return pltpu.make_async_remote_copy(
            src_ref=columns(h), dst_ref=columns(h), send_sem=sc.at[p], recv_sem=rc.at[p],
            device_id=sibling, device_id_type=MESH)

    for i in range(3):
        for d in range(2):
            gather.send(i, d, 0)
        if i == 0:
            for p in range(1, ny):
                started.append(y_copy(p, head))
                started[-1].start()
            started.append(core_copy(0, head))
            started[-1].start()

    def ring(i):
        for s in range(nz - 1):
            for d in range(2):
                gather.ring_step(i, d, s)

    def dots(i):
        tile = min(512, xs.shape[0])

        @pl.loop(0, xs.shape[0] // tile)
        def _(r):
            span = pl.ds(pl.multiple_of(r * tile, tile), tile)
            p_ref[i, span, :] = jnp.dot(xs[span, :], ws[i], preferred_element_type=F32).astype(BF16)

    ring(0)
    for p in range(1, ny):
        source = ((y + ny - p) % ny) * 2 + core
        y_copy(p, source).wait_recv()
        started.append(core_copy(p, source))
        started[-1].start()
    ring(1)
    for p in range(ny):
        core_copy(p, ((y + ny - p) % ny) * 2 + 1 - core).wait_recv()
    piece = min(256, width)

    @pl.loop(0, xs.shape[1] // piece)
    def _(r):
        span = pl.ds(pl.multiple_of(r * piece, piece), piece)
        xt_ref[span, :] = xs[:, span].T

    ring(2)
    for i in range(3):
        gather.wait_side(i)
        dots(i)
    gather.finish()
    for copy in started:
        copy.wait_send()


def project(inputs, master, nz, nx, nh):
    tokens, width = inputs.shape
    rows, cols = master.shape[1:]
    features = width * nh
    dma = pltpu.SemaphoreType.DMA
    ny = nh // 2
    vmem = pl.BlockSpec(memory_space=pltpu.VMEM)
    return pl.pallas_call(
        functools.partial(project_kernel, nz, nx, nh),
        out_shape=(jax.ShapeDtypeStruct((3, tokens, cols), BF16), jax.ShapeDtypeStruct((features, tokens), BF16)),
        in_specs=[vmem] * 2,
        out_specs=(vmem, vmem),
        scratch_shapes=[
            pltpu.VMEM((tokens, features), BF16),
            pltpu.VMEM((3, features, cols), BF16),
            dma((3, 2, nz - 1)), dma((3, 2, nz - 1)),
            dma((3, 2, nz, nx - 1)), dma((3, 2, nz, nx - 1)),
            dma((ny,)), dma((ny,)), dma((ny,)), dma((ny,)),
        ],
        compiler_params=pltpu.CompilerParams(collective_id=0, has_side_effects=True, vmem_limit_bytes=VMEM_LIMIT),
    )(inputs, master)


def update_kernel(nz, nx, xt_ref, g_ref, m_ref, m1_ref, m2_ref, out_ref,
                  own, xsend, xrecv, zsend, zrecv, ssx, rsx, ssz, rsz, sz, rz, sx, rx):
    rows = m_ref.shape[1]
    half = rows // 2
    tokens = g_ref.shape[1] * lax.axis_size("ctx")
    me = lax.axis_index("ctx")
    z, x = me // nx, me % nx
    gather = Gather(out_ref, nz, nx, rows, sz, rz, sx, rx)
    greet(ctx_peers(nz, nx))
    started = []

    def product(i, zb, xb):
        start = pl.multiple_of((zb * nx + xb) * rows, rows)
        return jnp.dot(xt_ref[pl.ds(start, rows), :], g_ref[i], preferred_element_type=F32)

    def x_copy(i, delta, p):
        return pltpu.make_async_remote_copy(
            src_ref=xsend.at[i, delta, p - 1], dst_ref=xrecv.at[i, delta, p - 1],
            send_sem=ssx.at[i, delta, p - 1], recv_sem=rsx.at[i, delta, p - 1],
            device_id={"ctx": z * nx + (x + p) % nx}, device_id_type=MESH)

    def z_copy(i, d, t):
        return pltpu.make_async_remote_copy(
            src_ref=zsend.at[i, d, t], dst_ref=zrecv.at[i, d, t],
            send_sem=ssz.at[i, d, t], recv_sem=rsz.at[i, d, t],
            device_id={"ctx": gather.ring_peer(d)}, device_id_type=MESH)

    order = []
    for k in range(1, nz // 2 + 1):
        order += [k] if k == nz - k else [k, nz - k]
    order.append(0)

    def partials(i):
        for delta in order:
            for p in range(1, nx):
                xsend[i, delta, p - 1] = product(i, (z + delta) % nz, (x + p) % nx).astype(BF16)
                started.append(x_copy(i, delta, p))
                started[-1].start()
        for delta in order:
            own[i, delta] = product(i, (z + delta) % nz, x)

    arrived = set()

    def reduce_step(i, d, t):
        delta = (nz - 1 - t) if d == 0 else (t + 1) % nz
        for p in range(1, nx):
            if (i, delta, p) not in arrived:
                arrived.add((i, delta, p))
                x_copy(i, delta, p).wait_recv()
        part = slice(d * half, (d + 1) * half)
        total = own[i, delta, part, :]
        for p in range(1, nx):
            total = total + xrecv[i, delta, p - 1, part, :].astype(F32)
        if t > 0:
            z_copy(i, d, t - 1).wait_recv()
            total = total + zrecv[i, d, t - 1].astype(F32)
        if t < nz - 1:
            zsend[i, d, t] = total.astype(BF16)
            started.append(z_copy(i, d, t))
            started[-1].start()
            return
        grad = total / tokens
        master = m_ref[i, part, :]
        first = 0.9 * m1_ref[i, part, :] + 0.1 * grad
        second = 0.95 * m2_ref[i, part, :] + 0.05 * grad * grad
        updated = master - 0.003 * (first / (jnp.sqrt(second) + 1e-08) + 0.1 * master)
        start = pl.multiple_of(me * rows + d * half, half)
        out_ref[i, pl.ds(start, half), :] = updated.astype(BF16)
        gather.send(i, d, 0)

    for i in range(3):
        partials(i)
    for i in range(4):
        for t in range(nz):
            for d in range(2):
                if i < 3:
                    reduce_step(i, d, t)
                if i > 0 and t < nz - 1:
                    gather.ring_step(i - 1, d, t)
    for i in range(3):
        gather.wait_side(i)
    gather.finish()
    for copy in started:
        copy.wait_send()


def update(xt, grads, master, moment_one, moment_two, nz, nx):
    rows, cols = master.shape[1:]
    dma = pltpu.SemaphoreType.DMA
    vmem = pl.BlockSpec(memory_space=pltpu.VMEM)
    return pl.pallas_call(
        functools.partial(update_kernel, nz, nx),
        out_shape=jax.ShapeDtypeStruct((3, xt.shape[0], cols), BF16),
        in_specs=[vmem] * 5,
        out_specs=vmem,
        scratch_shapes=[
            pltpu.VMEM((3, nz, rows, cols), F32),
            pltpu.VMEM((3, nz, nx - 1, rows, cols), BF16),
            pltpu.VMEM((3, nz, nx - 1, rows, cols), BF16),
            pltpu.VMEM((3, 2, nz - 1, rows // 2, cols), BF16),
            pltpu.VMEM((3, 2, nz - 1, rows // 2, cols), BF16),
            dma((3, nz, nx - 1)), dma((3, nz, nx - 1)),
            dma((3, 2, nz - 1)), dma((3, 2, nz - 1)),
            dma((3, 2, nz - 1)), dma((3, 2, nz - 1)),
            dma((3, 2, nz, nx - 1)), dma((3, 2, nz, nx - 1)),
        ],
        compiler_params=pltpu.CompilerParams(collective_id=1, has_side_effects=True, vmem_limit_bytes=VMEM_LIMIT),
    )(xt, grads, master, moment_one, moment_two)


def dot_t(a, b):
    return lax.dot_general(a, b, (((0,), (0,)), ((), ())), preferred_element_type=F32)


def dot_nt(a, b):
    return lax.dot_general(a, b, (((1,), (1,)), ((), ())), preferred_element_type=F32)


def states_kernel(scale, depth, p_ref, g_ref, f_ref, own_ref, pend_ref):
    queries = p_ref[0]
    own_ref[0] = dot_t(p_ref[1], p_ref[2])
    grads = g_ref[...].astype(F32)
    for level in range(depth):
        weighted = (f_ref[0, :, LV_IN + level:LV_IN + level + 1] * grads).astype(BF16)
        pend_ref[level, 0] = scale * dot_t(queries, weighted)


def inner_kernel(scale, tile, p_ref, g_ref, f_ref, att_ref, dq_ref, dk_ref, dv_ref):
    tokens = g_ref.shape[0]
    top = f_ref[0, :, LV_IN - 1:LV_IN]
    row = lax.broadcasted_iota(jnp.int32, (tile, tile), 0)
    col = lax.broadcasted_iota(jnp.int32, (tile, tile), 1)
    crossed = jnp.bitwise_xor(row, col)
    causal = row >= col
    for b in range(tokens // tile):
        span = slice(b * tile, (b + 1) * tile)
        queries, grads = p_ref[0, span, :], g_ref[span, :]
        weights = jnp.broadcast_to(f_ref[0, span, 0:1], (tile, tile))
        for level in range(1, LV_IN):
            factor = f_ref[0, span, level:level + 1]
            weights = jnp.where(crossed >= 1 << (level - 1), factor, weights)
        weights = jnp.where(causal, weights, 0.0)
        rest = top[span]
        if b:
            weights = jnp.concatenate([jnp.broadcast_to(rest, (tile, b * tile)), weights], axis=1)
        seen = slice(0, (b + 1) * tile)
        keys, values = p_ref[1, seen, :], p_ref[2, seen, :]
        probs = (scale * dot_nt(queries, keys) * weights).astype(BF16)
        mixed = (scale * dot_nt(grads, values) * weights).astype(BF16)
        att_ref[span, :] = jnp.dot(probs, values, preferred_element_type=F32)
        dq_ref[span, :] = jnp.dot(mixed, keys, preferred_element_type=F32)
        to_keys = dot_t(mixed, queries)
        to_values = dot_t(probs, grads)
        if b:
            before = slice(0, b * tile)
            dk_ref[before, :] += to_keys[before]
            dv_ref[before, :] += to_values[before]
        dk_ref[span, :] = to_keys[b * tile:]
        dv_ref[span, :] = to_values[b * tile:]


def outer_kernel(scale, depth, p_ref, g_ref, f_ref, b_ref, i_ref, att_ref, dq_ref, dk_ref, dv_ref, out_ref, grad_ref):
    queries, grads = p_ref[0], g_ref[...]
    outer = jnp.zeros(att_ref.shape, F32)
    back = jnp.zeros(att_ref.shape, F32)
    for level in range(depth):
        factor = f_ref[0, :, LV_IN + level:LV_IN + level + 1]
        outer = outer + factor * jnp.dot(queries, b_ref[level, 0], preferred_element_type=F32)
        back = back + factor * dot_nt(grads, b_ref[level, 0])
    out_ref[...] = (att_ref[...] + scale * outer).astype(BF16)
    grad_ref[0] = (dq_ref[...] + scale * back).astype(BF16)
    grad_ref[1] = (dk_ref[...] + dot_nt(p_ref[2], i_ref[0])).astype(BF16)
    grad_ref[2] = (dv_ref[...] + jnp.dot(p_ref[1], i_ref[0], preferred_element_type=F32)).astype(BF16)


def from_partner(value, axis, apart):
    mask = 2**apart
    pairs = [(source, source ^ mask) for source in range(lax.axis_size(axis))]
    return lax.ppermute(value, axis, pairs)


def body(inputs, level_factors, out_grad, master, moment_one, moment_two):
    tokens_dev = inputs.shape[0]
    heads = level_factors.shape[0]
    head_size = out_grad.shape[1] // heads
    levels = level_factors.shape[1]
    block_index = lax.axis_index("ctx")
    blocks = lax.axis_size("ctx")
    nz, nx = factor_ctx(blocks)
    depth = min(blocks.bit_length() - 1, levels - LV_IN)
    scale = 1.0 / math.sqrt(head_size * tokens_dev)
    factors = jnp.transpose(level_factors, (0, 2, 1))
    projected, xt = project(inputs, master, nz, nx, lax.axis_size("head"))

    p_spec = pl.BlockSpec((3, tokens_dev, head_size), lambda h: (0, 0, h))
    g_spec = pl.BlockSpec((tokens_dev, head_size), lambda h: (0, h))
    f_spec = pl.BlockSpec((1, tokens_dev, levels), lambda h: (h, 0, 0))
    s_spec = pl.BlockSpec((1, head_size, head_size), lambda h: (h, 0, 0))
    l_spec = pl.BlockSpec((depth, 1, head_size, head_size), lambda h: (0, h, 0, 0))
    params = pltpu.CompilerParams(vmem_limit_bytes=VMEM_LIMIT)
    wide = jax.ShapeDtypeStruct((tokens_dev, heads * head_size), F32)
    narrow = jax.ShapeDtypeStruct((tokens_dev, heads * head_size), BF16)
    own_state, pending = pl.pallas_call(
        functools.partial(states_kernel, scale, depth),
        grid=(heads,),
        out_shape=(jax.ShapeDtypeStruct((heads, head_size, head_size), F32),
                   jax.ShapeDtypeStruct((depth, heads, head_size, head_size), F32)),
        in_specs=[p_spec, g_spec, f_spec],
        out_specs=(s_spec, l_spec),
        compiler_params=params,
    )(projected, out_grad, factors)

    square = tokens_dev * tokens_dev * head_size * heads
    inner, dq, dk, dv = pl.pallas_call(
        functools.partial(inner_kernel, scale, min(256, tokens_dev)),
        grid=(heads,),
        out_shape=(wide,) * 4,
        in_specs=[p_spec, g_spec, f_spec],
        out_specs=(g_spec,) * 4,
        compiler_params=params,
        cost_estimate=pl.CostEstimate(flops=12 * square, bytes_accessed=24 * tokens_dev * heads * head_size, transcendentals=0),
    )(projected, out_grad, factors)

    running = own_state
    buckets = []
    for level in range(depth):
        other = from_partner(running, "ctx", level)
        upper = (block_index >> level & 1) == 1
        buckets.append(jnp.where(upper, other, 0.0).astype(BF16))
        running = running + other
    buckets_b = jnp.stack(buckets)
    incoming = jnp.zeros((heads, head_size, head_size), F32)
    for level in range(depth):
        partner = from_partner(pending[level:depth].astype(BF16), "ctx", level).astype(F32)
        lower = (block_index >> level & 1) == 0
        incoming = incoming + jnp.where(lower, partner[0], 0.0)
        if level + 1 < depth:
            pending = pending.at[level + 1:depth].add(partner[1:])
    incoming_b = incoming.astype(BF16)

    attention, grads = pl.pallas_call(
        functools.partial(outer_kernel, scale, depth),
        grid=(heads,),
        out_shape=(narrow, jax.ShapeDtypeStruct((3, tokens_dev, heads * head_size), BF16)),
        in_specs=[p_spec, g_spec, f_spec, l_spec, s_spec] + [g_spec] * 4,
        out_specs=(g_spec, p_spec),
        compiler_params=params,
    )(projected, out_grad, factors, buckets_b, incoming_b, inner, dq, dk, dv)

    new_weights = update(xt, grads, master, moment_one, moment_two, nz, nx)
    return (attention, new_weights)


def solution(mesh):
    placed = (
        P("ctx", "head"),
        P("head", None, "ctx"),
        P("ctx", "head"),
        P(None, "ctx", "head"),
        P(None, "ctx", "head"),
        P(None, "ctx", "head"),
    )
    return jax.shard_map(
        body,
        mesh=mesh,
        in_specs=placed,
        out_specs=(P("ctx", "head"), P(None, None, "head")),
        check_vma=False,
    )
```

time: 502 us -> 293 us (0.58); the launches traced: 493 us -> 291 us
  waiting for transfers between devices: 331 us -> 19.1 us
  Pallas kernels: 0 us -> 255 us
  matrix products: 94.9 us -> 0 us
  other arithmetic: 30.4 us -> 3.06 us
  between operations: 14.7 us -> 0.73 us
  local copies, waits for them, and re-layouts: 19.6 us -> 9.33 us
    pallas_call x0 -> x5, Pallas kernels: none -> 255 us  [the longest x1 145 us: update(): pl.pallas_call(functools.partial(update_kernel, nz, nx), out_shape=jax.Sh...]
    all_gather x4 -> x0, waiting for transfers between devices: 200 us -> none  [the longest x1 104 us: body(): lax.all_gather(shard_b, 'ctx', axis=1, tiled=True)]
    reduce_scatter x1 -> x0, waiting for transfers between devices: 117 us -> none  [body(): lax.psum_scatter(jnp.einsum('tr,tc->rc', whole, grad_joined, preferred_el...]
    dot_general x15 -> x0, matrix products: 94.9 us -> none  [the longest x1 21.5 us: body(): jnp.einsum('htd,hsd->hts', queries_b, keys_b, preferred_element_type=jnp....]
    eq x4 -> x0, other arithmetic: 20.6 us -> none  [inner_weights(): levels == level]
    ppermute x3 -> x6, waiting for transfers between devices: 12.2 us -> 19.1 us  [from_partner(): return lax.ppermute(value, axis, pairs)]
    unnamed x45 -> x6, local copies, waits for them, and re-layouts: 10.9 us -> 9.33 us
  transfers between devices with their start and end apart: 8 -> 6, of which waited for: 6 -> 4; matrix products, arithmetic and copies ran while one was open for 18% -> 1% of each run, Pallas kernels for 0% -> 5%
where the time goes in v1:
time: 293 us; the launch traced here: 291 us
  Pallas kernels  255 us (87%)
  waiting for transfers between devices  19.1 us (7%)
  local copies, waits for them, and re-layouts  9.33 us (3%)
  starting transfers between devices  3.96 us (1%)
  other arithmetic  3.06 us (1%)
    pallas_call x1, Pallas kernels, update(): pl.pallas_call(functools.partial(update_kernel, nz, nx), out_shape=jax.Sh...  145 us
    pallas_call x1, Pallas kernels, project(): pl.pallas_call(functools.partial(project_kernel, nz, nx, nh), out_shape=(...  81.1 us
    ppermute x6, waiting for transfers between devices, from_partner(): return lax.ppermute(value, axis, pairs)  19.1 us
    pallas_call x1, Pallas kernels, body(): pl.pallas_call(functools.partial(inner_kernel, scale, min(256, tokens_dev...  13.7 us
    unnamed x6, local copies, waits for them, and re-layouts  9.33 us
    pallas_call x1, Pallas kernels, body(): pl.pallas_call(functools.partial(outer_kernel, scale, depth), grid=(heads...  8.51 us
    pallas_call x1, Pallas kernels, body(): pl.pallas_call(functools.partial(states_kernel, scale, depth), grid=(head...  6.17 us
  transfers between devices with their start and end apart: 6, of which 4 were waited for; matrix products, arithmetic and copies ran while one was open for 1% of the time, Pallas kernels for 5%

profile of v1, /device:TPU:4, one launch (start us, length us, event | category | flops | bytes accessed | tf_op | source)
XLA Modules:
  0.0 291.0 jit_solution(3174418424296512532)
XLA Ops:
  0.6 3.0 %copy.8 = f32[4,13,1024]{1,2,0:T(8,128)} copy(f32[4,13,1024]{2,0,1:T(4,128)} %param.11) | data formatting | bytes 425984 | tf_op args[1]
  3.6 81.1 %shard_map.77 = (bf16[3,1024,512]{2,1,0:T(8,128)(2,1)}, bf16[2048,1024]{1,0:T(8,128)(2,1)}) custom-call(bf16[1024,512]{1,0:T(8,128)(2,1)} %x_ref.1, f32[3,256,512]{2,1,0:T(8,128)} %m_ref.3), custom_call_target="tpu_custom_call" | custom-call | tf_op jit(solution)/shard_map/pallas_call | solution.py:180
  84.7 6.2 %shard_map.78 = (f32[4,128,128]{2,1,0:T(8,128)}, f32[3,4,128,128]{3,2,1,0:T(8,128)}) custom-call(bf16[3,1024,512]{2,1,0:T(8,128)(2,1)} %get-tuple-element.36.p_ref, bf16[1024,512]{1,0:T(8,128)(2,1)} %g_ref.5, f32[4,1024,13]{2,1,0:T(8,128)} %bitcast.9), custom_call_target="tpu_custom_call" | custom-call | tf_op jit(solution)/shard_map/pallas_call | solution.py:398
  90.9 0.5 collective-permute-start
  91.4 1.2 convert_element_type.35
  92.6 0.0 copy-start.1
  92.6 1.6 collective-permute-start.3
  94.2 13.7 %shard_map.79 = (f32[1024,512]{1,0:T(8,128)}, f32[1024,512]{1,0:T(8,128)}, f32[1024,512]{1,0:T(8,128)}, f32[1024,512]{1,0:T(8,128)}) custom-call(bf16[3,1024,512]{2,1,0:T(8,128)(2,1)} %get-tuple-element.36.p_ref, bf16[1024,512]{1,0:T(8,128)(2,1)} %g_ref.5, f32[4,1024,13]{2,1,0:T(8,128)} %bitcast.10), custom_call_target="tpu_custom_call" | custom-call | flops 6442450944 | bytes 12582912 | tf_op jit(solution)/shard_map/pallas_call | solution.py:409
  107.9 0.6 collective-permute-start.1
  108.5 0.1 convert_element_type.36
  108.5 0.4 copy-done
  109.0 0.1 fusion.8
  109.1 1.2 collective-permute-start.4
  110.3 8.4 %collective-permute-done.1 = f32[4,128,128]{2,1,0:T(8,128)S(1)} collective-permute-done((f32[4,128,128]{2,1,0:T(8,128)S(1)}, f32[4,128,128]{2,1,0:T(8,128)S(1)}, u32[]{:S(2)}, u32[]{:S(2)}) %collective-permute-start.1) | collective-permute-done | bytes 262176 | tf_op jit(solution)/shard_map/ppermute | solution.py:374
  118.7 0.1 collective-permute-start.2
  118.8 3.0 %collective-permute-done.4 = bf16[2,4,128,128]{3,2,1,0:T(8,128)(2,1)S(1)} collective-permute-done((bf16[2,4,128,128]{3,2,1,0:T(8,128)(2,1)S(1)}, bf16[2,4,128,128]{3,2,1,0:T(8,128)(2,1)S(1)}, u32[]{:S(2)}, u32[]{:S(2)}) %collective-permute-start.4) | collective-permute-done | bytes 262176 | tf_op jit(solution)/shard_map/ppermute | solution.py:374
  121.9 0.1 collective-permute-start.5
  121.9 7.1 %collective-permute-done.2 = bf16[4,128,128]{2,1,0:T(8,128)(2,1)S(1)} collective-permute-done((bf16[4,128,128]{2,1,0:T(8,128)(2,1)S(1)}, bf16[4,128,128]{2,1,0:T(8,128)(2,1)S(1)}, u32[]{:S(2)}, u32[]{:S(2)}) %collective-permute-start.2) | collective-permute-done | bytes 131104 | tf_op jit(solution)/shard_map/ppermute | solution.py:374
  129.1 0.8 pad_maximum_fusion.b_ref
  129.9 0.6 collective-permute-done.5
  130.5 0.7 fusion.7.i_ref
  131.2 8.5 %shard_map.80 = (bf16[1024,512]{1,0:T(8,128)(2,1)}, bf16[3,1024,512]{2,1,0:T(8,128)(2,1)}) custom-call(bf16[3,1024,512]{2,1,0:T(8,128)(2,1)} %get-tuple-element.36.p_ref, bf16[1024,512]{1,0:T(8,128)(2,1)} %g_ref.5, f32[4,1024,13]{2,1,0:T(8,128)} %bitcast.11, bf16[3,4,128,128]{3,2,1,0:T(8,128)(2,1)} %pad_maximum_fusion.b_ref, ...), custom_call_target="tpu_custom_call" | custom-call | tf_op jit(solution)/shard_map/pallas_call | solution.py:436
  139.7 145.4 %shard_map.81 = bf16[3,2048,512]{2,1,0:T(8,128)(2,1)} custom-call(bf16[2048,1024]{1,0:T(8,128)(2,1)} %get-tuple-element.44.xt_ref, bf16[3,1024,512]{2,1,0:T(8,128)(2,1)} %get-tuple-element.45.g_ref, f32[3,256,512]{2,1,0:T(8,128)} %m_ref.3, f32[3,256,512]{2,1,0:T(8,128)} %m1_ref.1, f32[3,256,512]{2,1,0:T(8,128)} %m2_ref.1), custom_call_target="tpu_custom_call" | custom-call | tf_op jit(solution)/shard_map/pallas_call | solution.py:286
  285.1 5.9 %copy.10 = bf16[3,2048,512]{2,1,0:T(8,128)(2,1)} copy(bf16[3,2048,512]{2,1,0:T(8,128)(2,1)} %shard_map.81) | data formatting | bytes 12582912
  (10 shorter events, 0.2 us)
Async XLA Ops:
  90.9 17.0 %collective-permute-start = (f32[4,128,128]{2,1,0:T(8,128)}, f32[4,128,128]{2,1,0:T(8,128)S(1)}, u32[]{:S(2)}, u32[]{:S(2)}) collective-permute-start(f32[4,128,128]{2,1,0:T(8,128)} %get-tuple-element.37), channel_id=1, source_target_pairs={{0,4},{4,0},{8,12},{12,8},{16,20},{20,16},{24,28},{28,24},{1,5},{5... | collective-permute-start | bytes 786440 | tf_op jit(solution)/shard_map/ppermute | solution.py:374
  92.6 15.3 %copy-start.1 = (f32[4,128,128]{2,1,0:T(8,128)S(1)}, f32[4,128,128]{2,1,0:T(8,128)}, u32[]{:S(2)}) copy-start(f32[4,128,128]{2,1,0:T(8,128)} %get-tuple-element.37) | copy-start | bytes 786436
  92.6 15.8 %collective-permute-start.3 = (bf16[3,4,128,128]{3,2,1,0:T(8,128)(2,1)S(1)}, bf16[3,4,128,128]{3,2,1,0:T(8,128)(2,1)S(1)}, u32[]{:S(2)}, u32[]{:S(2)}) collective-permute-start(bf16[3,4,128,128]{3,2,1,0:T(8,128)(2,1)S(1)} %convert_element_type.35), channel_id=1, source_target_pairs={{0,4},{4,0},{8,12},{12,8},{16,20},{20,16},{24,28},{28,24},{1,5},{5... | collective-permute-start | bytes 1179656 | tf_op jit(solution)/shard_map/ppermute | solution.py:374
  107.9 1.1 copy-start
  107.9 10.7 %collective-permute-start.1 = (f32[4,128,128]{2,1,0:T(8,128)S(1)}, f32[4,128,128]{2,1,0:T(8,128)S(1)}, u32[]{:S(2)}, u32[]{:S(2)}) collective-permute-start(f32[4,128,128]{2,1,0:T(8,128)S(1)} %add.28), channel_id=1, source_target_pairs={{0,8},{4,12},{8,0},{12,4},{16,24},{20,28},{24,16},{28,20},{1,9},{5... | collective-permute-start | bytes 786440 | tf_op jit(solution)/shard_map/ppermute | solution.py:374
  109.1 12.7 %collective-permute-start.4 = (bf16[2,4,128,128]{3,2,1,0:T(8,128)(2,1)S(1)}, bf16[2,4,128,128]{3,2,1,0:T(8,128)(2,1)S(1)}, u32[]{:S(2)}, u32[]{:S(2)}) collective-permute-start(bf16[2,4,128,128]{3,2,1,0:T(8,128)(2,1)S(1)} %get-tuple-element.46), channel_id=1, source_target_pairs={{0,8},{4,12},{8,0},{12,4},{16,24},{20,28},{24,16},{28,20},{1,9},{5... | collective-permute-start | bytes 786440 | tf_op jit(solution)/shard_map/ppermute | solution.py:374
  118.7 10.4 %collective-permute-start.2 = (bf16[4,128,128]{2,1,0:T(8,128)(2,1)S(1)}, bf16[4,128,128]{2,1,0:T(8,128)(2,1)S(1)}, u32[]{:S(2)}, u32[]{:S(2)}) collective-permute-start(bf16[4,128,128]{2,1,0:T(8,128)(2,1)S(1)} %get-tuple-element.49), channel_id=1, source_target_pairs={{0,16},{4,20},{8,24},{12,28},{16,0},{20,4},{24,8},{28,12},{1,17},{... | collective-permute-start | bytes 393224 | tf_op jit(solution)/shard_map/ppermute | solution.py:374
  121.9 8.6 %collective-permute-start.5 = (bf16[1,4,128,128]{3,2,1,0:T(8,128)(2,1)S(1)}, bf16[1,4,128,128]{3,2,1,0:T(8,128)(2,1)S(1)}, u32[]{:S(2)}, u32[]{:S(2)}) collective-permute-start(bf16[1,4,128,128]{3,2,1,0:T(8,128)(2,1)S(1)} %fusion), channel_id=1, source_target_pairs={{0,16},{4,20},{8,24},{12,28},{16,0},{20,4},{24,8},{28,12},{1,17},{... | collective-permute-start | bytes 393224 | tf_op jit(solution)/shard_map/ppermute | solution.py:374

commit v2 on v1

v2 whole, which is shorter than its diff:
```python
import functools
import math

import jax
import jax.numpy as jnp
from jax import lax
from jax.experimental import pallas as pl
from jax.experimental.pallas import tpu as pltpu
from jax.sharding import PartitionSpec as P

LV_IN = 8
MESH = pl.DeviceIdType.MESH
WIDE = ((1, 1),)
F32 = jnp.float32
BF16 = jnp.bfloat16
VMEM_LIMIT = 60 * 1024 * 1024


def factor_ctx(count):
    nx = 1 << ((count.bit_length() - 1) // 2)
    return count // nx, nx


class Gather:
    def __init__(self, ref, nz, nx, rows, sz, rz, sx, rx):
        self.ref, self.nz, self.nx, self.rows = ref, nz, nx, rows
        self.sz, self.rz, self.sx, self.rx = sz, rz, sx, rx
        me = lax.axis_index("ctx")
        self.z, self.x = me // nx, me % nx
        self.started = []

    def piece(self, i, d, z, x):
        half = self.rows // 2
        start = pl.multiple_of((z * self.nx + x) * self.rows + d * half, half)
        return self.ref.at[i, pl.ds(start, half), :]

    def origin(self, d, t):
        return (self.z + (self.nz - t if d == 0 else t)) % self.nz

    def ring_peer(self, d):
        return ((self.z + (1 if d == 0 else self.nz - 1)) % self.nz) * self.nx + self.x

    def ring_copy(self, i, d, s, z, q):
        view = self.piece(i, d, z, (self.x + q) % self.nx)
        return pltpu.make_async_remote_copy(
            src_ref=view, dst_ref=view, send_sem=self.sz.at[i, d, s, q], recv_sem=self.rz.at[i, d, s, q],
            device_id={"ctx": self.ring_peer(d)}, device_id_type=MESH)

    def side_copy(self, i, d, t, p, x):
        view = self.piece(i, d, self.origin(d, t), x)
        return pltpu.make_async_remote_copy(
            src_ref=view, dst_ref=view, send_sem=self.sx.at[i, d, t, p - 1], recv_sem=self.rx.at[i, d, t, p - 1],
            device_id={"ctx": self.z * self.nx + (self.x + p) % self.nx}, device_id_type=MESH)

    def start(self, copy):
        copy.start()
        self.started.append(copy)

    def send(self, i, d, t):
        if t < self.nz - 1:
            self.start(self.ring_copy(i, d, t, self.origin(d, t), 0))
        for p in range(1, self.nx):
            self.start(self.side_copy(i, d, t, p, self.x))

    def inject(self, i, d):
        for p in range(1, self.nx):
            self.side_copy(i, d, 0, p, (self.x + self.nx - p) % self.nx).wait_recv()
            self.start(self.ring_copy(i, d, 0, self.z, self.nx - p))

    def ring_step(self, i, d, s):
        wide = (i, d) in WIDE
        if wide and s == 0:
            self.inject(i, d)
        for q in range(self.nx if wide else 1):
            self.ring_copy(i, d, s, self.origin(d, s + 1), q).wait_recv()
            if wide and s + 1 < self.nz - 1:
                self.start(self.ring_copy(i, d, s + 1, self.origin(d, s + 1), q))
        if not wide:
            self.send(i, d, s + 1)

    def wait_side(self, i):
        for t in range(self.nz):
            for d in range(2):
                if (i, d) not in WIDE:
                    for p in range(1, self.nx):
                        self.side_copy(i, d, t, p, (self.x + self.nx - p) % self.nx).wait_recv()

    def finish(self):
        for copy in self.started:
            copy.wait_send()


def ctx_peers(nz, nx):
    me = lax.axis_index("ctx")
    z, x = me // nx, me % nx
    peers = [{"ctx": ((z + 1) % nz) * nx + x}, {"ctx": ((z + nz - 1) % nz) * nx + x}]
    peers += [{"ctx": z * nx + (x + p) % nx} for p in range(1, nx)]
    return peers


def greet(peers):
    barrier = pltpu.get_barrier_semaphore()
    for peer in peers:
        pl.semaphore_signal(barrier, inc=1, device_id=peer, device_id_type=MESH)
    pl.semaphore_wait(barrier, len(peers))


def project_kernel(nz, nx, nh, x_ref, m_ref, f_ref, p_ref, xt_ref, ft_ref, xs, ws, sz, rz, sx, rx, sy, ry, sc, rc):
    rows = m_ref.shape[1]
    width = x_ref.shape[1]
    ny = nh // 2
    head = lax.axis_index("head")
    y, core = head // 2, head % 2
    sibling = {"head": y * 2 + 1 - core}
    peers = ctx_peers(nz, nx) + [sibling]
    peers += [{"head": ((y + p) % ny) * 2 + core} for p in range(1, ny)]
    gather = Gather(ws, nz, nx, rows, sz, rz, sx, rx)
    own = pl.multiple_of(lax.axis_index("ctx") * rows, rows)
    for i in range(3):
        ws[i, pl.ds(own, rows), :] = m_ref[i].astype(BF16)

    def columns(h):
        return xs.at[:, pl.ds(pl.multiple_of(h * width, width), width)]

    greet(peers)
    xs[:, pl.ds(pl.multiple_of(head * width, width), width)] = x_ref[...]
    started = []

    def y_copy(p, h):
        return pltpu.make_async_remote_copy(
            src_ref=columns(h), dst_ref=columns(h), send_sem=sy.at[p], recv_sem=ry.at[p],
            device_id={"head": ((y + p) % ny) * 2 + core}, device_id_type=MESH)

    def core_copy(p, h):
        return pltpu.make_async_remote_copy(
            src_ref=columns(h), dst_ref=columns(h), send_sem=sc.at[p], recv_sem=rc.at[p],
            device_id=sibling, device_id_type=MESH)

    for i in range(3):
        for d in range(2):
            gather.send(i, d, 0)
        if i == 0:
            for p in range(1, ny):
                started.append(y_copy(p, head))
                started[-1].start()
            started.append(core_copy(0, head))
            started[-1].start()

    def ring(i):
        for s in range(nz - 1):
            for d in range(2):
                gather.ring_step(i, d, s)

    def dots(i):
        tile = min(512, xs.shape[0])

        @pl.loop(0, xs.shape[0] // tile)
        def _(r):
            span = pl.ds(pl.multiple_of(r * tile, tile), tile)
            p_ref[i, span, :] = jnp.dot(xs[span, :], ws[i], preferred_element_type=F32).astype(BF16)

    for h in range(f_ref.shape[0]):
        ft_ref[h] = f_ref[h].T
    ring(0)
    for p in range(1, ny):
        source = ((y + ny - p) % ny) * 2 + core
        y_copy(p, source).wait_recv()
        started.append(core_copy(p, source))
        started[-1].start()
    ring(1)
    for p in range(ny):
        core_copy(p, ((y + ny - p) % ny) * 2 + 1 - core).wait_recv()
    piece = min(256, width)

    @pl.loop(0, xs.shape[1] // piece)
    def _(r):
        span = pl.ds(pl.multiple_of(r * piece, piece), piece)
        xt_ref[span, :] = xs[:, span].T

    ring(2)
    for i in range(3):
        gather.wait_side(i)
        dots(i)
    gather.finish()
    for copy in started:
        copy.wait_send()


def project(inputs, master, factors, nz, nx, nh):
    tokens, width = inputs.shape
    rows, cols = master.shape[1:]
    features = width * nh
    dma = pltpu.SemaphoreType.DMA
    ny = nh // 2
    vmem = pl.BlockSpec(memory_space=pltpu.VMEM)
    return pl.pallas_call(
        functools.partial(project_kernel, nz, nx, nh),
        out_shape=(jax.ShapeDtypeStruct((3, tokens, cols), BF16), jax.ShapeDtypeStruct((features, tokens), BF16),
                   jax.ShapeDtypeStruct((factors.shape[0], tokens, factors.shape[1]), F32)),
        in_specs=[vmem] * 3,
        out_specs=(vmem,) * 3,
        scratch_shapes=[
            pltpu.VMEM((tokens, features), BF16),
            pltpu.VMEM((3, features, cols), BF16),
            dma((3, 2, nz - 1, nx)), dma((3, 2, nz - 1, nx)),
            dma((3, 2, nz, nx - 1)), dma((3, 2, nz, nx - 1)),
            dma((ny,)), dma((ny,)), dma((ny,)), dma((ny,)),
        ],
        compiler_params=pltpu.CompilerParams(collective_id=0, has_side_effects=True, vmem_limit_bytes=VMEM_LIMIT),
    )(inputs, master, factors)


def dot_t(a, b):
    return lax.dot_general(a, b, (((0,), (0,)), ((), ())), preferred_element_type=F32)


def dot_nt(a, b):
    return lax.dot_general(a, b, (((1,), (1,)), ((), ())), preferred_element_type=F32)


def inner_head(scale, tile, size, h, p_ref, g_ref, f_ref, acc):
    tokens = g_ref.shape[0]
    lane = pl.ds(pl.multiple_of(h * size, size), size)
    row = lax.broadcasted_iota(jnp.int32, (tile, tile), 0)
    col = lax.broadcasted_iota(jnp.int32, (tile, tile), 1)
    crossed = jnp.bitwise_xor(row, col)
    causal = row >= col
    for b in range(tokens // tile):
        span = slice(b * tile, (b + 1) * tile)
        queries, grads = p_ref[0, span, lane], g_ref[span, lane]
        weights = jnp.broadcast_to(f_ref[h, span, 0:1], (tile, tile))
        for level in range(1, LV_IN):
            factor = f_ref[h, span, level:level + 1]
            weights = jnp.where(crossed >= 1 << (level - 1), factor, weights)
        weights = jnp.where(causal, weights, 0.0)
        if b:
            rest = f_ref[h, span, LV_IN - 1:LV_IN]
            weights = jnp.concatenate([jnp.broadcast_to(rest, (tile, b * tile)), weights], axis=1)
        seen = slice(0, (b + 1) * tile)
        keys, values = p_ref[1, seen, lane], p_ref[2, seen, lane]
        probs = (scale * dot_nt(queries, keys) * weights).astype(BF16)
        mixed = (scale * dot_nt(grads, values) * weights).astype(BF16)
        acc[0, span, lane] = jnp.dot(probs, values, preferred_element_type=F32)
        acc[1, span, lane] = jnp.dot(mixed, keys, preferred_element_type=F32)
        to_keys = dot_t(mixed, queries)
        to_values = dot_t(probs, grads)
        if b:
            before = slice(0, b * tile)
            acc[2, before, lane] += to_keys[before]
            acc[3, before, lane] += to_values[before]
        acc[2, span, lane] = to_keys[b * tile:]
        acc[3, span, lane] = to_values[b * tile:]


def update_kernel(nz, nx, scale, depth, p_ref, g_ref, f_ref, xt_ref, m_ref, m1_ref, m2_ref, att_ref, out_ref,
                  acc, dy, sums, pend, sum_out, sum_in, pend_out, pend_in,
                  own, xsend, xrecv, zsend, zrecv, sse, rse, spe, rpe, ssx, rsx, ssz, rsz, sz, rz, sx, rx):
    rows = m_ref.shape[1]
    half = rows // 2
    heads = f_ref.shape[0]
    size = g_ref.shape[1] // heads
    tokens = g_ref.shape[0] * lax.axis_size("ctx")
    me = lax.axis_index("ctx")
    z, x = me // nx, me % nx
    gather = Gather(out_ref, nz, nx, rows, sz, rz, sx, rx)

    def partner(level):
        mask = 1 << level
        return {"ctx": me + mask - 2 * mask * (me // mask % 2)}

    greet(ctx_peers(nz, nx) + [partner(level) for level in range(depth)])
    started = []

    def exchange(level):
        return [
            pltpu.make_async_remote_copy(
                src_ref=sum_out.at[level], dst_ref=sum_in.at[level], send_sem=sse.at[level], recv_sem=rse.at[level],
                device_id=partner(level), device_id_type=MESH),
            pltpu.make_async_remote_copy(
                src_ref=pend_out.at[level, pl.ds(level, depth - level)],
                dst_ref=pend_in.at[level, pl.ds(level, depth - level)],
                send_sem=spe.at[level], recv_sem=rpe.at[level],
                device_id=partner(level), device_id_type=MESH)]

    def exchange_start(level):
        sum_out[level] = sums[...]
        pend_out[level, level:] = pend[level:].astype(BF16)
        for copy in exchange(level):
            copy.start()

    def exchange_end(level):
        for copy in exchange(level):
            copy.wait_recv()
        if level + 1 < depth:
            sums[...] += sum_in[level]
            pend[level + 1:] += pend_in[level, level + 1:].astype(F32)
            exchange_start(level + 1)

    @pl.loop(0, heads)
    def _(h):
        lane = pl.ds(pl.multiple_of(h * size, size), size)
        queries = p_ref[0, :, lane]
        sums[h] = dot_t(p_ref[1, :, lane], p_ref[2, :, lane])
        grads = g_ref[:, lane].astype(F32)
        for level in range(depth):
            weighted = (f_ref[h, :, LV_IN + level:LV_IN + level + 1] * grads).astype(BF16)
            pend[level, h] = scale * dot_t(queries, weighted)

    exchange_start(0)

    @pl.loop(0, heads)
    def _(h):
        inner_head(scale, min(256, g_ref.shape[0]), size, h, p_ref, g_ref, f_ref, acc)
        for level in range(depth):
            @pl.when(h == min(level, heads - 1))
            def _():
                exchange_end(level)

    @pl.loop(0, heads)
    def _(h):
        lane = pl.ds(pl.multiple_of(h * size, size), size)
        queries, grads = p_ref[0, :, lane], g_ref[:, lane]
        outer = jnp.zeros(queries.shape, F32)
        back = jnp.zeros(queries.shape, F32)
        for level in range(depth):
            factor = f_ref[h, :, LV_IN + level:LV_IN + level + 1]
            upper = jnp.full((size, size), (me >> level) & 1) == 1
            bucket = jnp.where(upper, sum_in[level, h], 0.0).astype(BF16)
            outer = outer + factor * jnp.dot(queries, bucket, preferred_element_type=F32)
            back = back + factor * dot_nt(grads, bucket)
        att_ref[:, lane] = (acc[0, :, lane] + scale * outer).astype(BF16)
        dy[0, :, lane] = (acc[1, :, lane] + scale * back).astype(BF16)

    def key_value_grads():
        @pl.loop(0, heads)
        def _(h):
            lane = pl.ds(pl.multiple_of(h * size, size), size)
            incoming = jnp.zeros((size, size), F32)
            for level in range(depth):
                lower = jnp.full((size, size), (me >> level) & 1) == 0
                incoming = incoming + jnp.where(lower, pend_in[level, level, h].astype(F32), 0.0)
            incoming = incoming.astype(BF16)
            dy[1, :, lane] = (acc[2, :, lane] + dot_nt(p_ref[2, :, lane], incoming)).astype(BF16)
            dy[2, :, lane] = (acc[3, :, lane] + jnp.dot(
                p_ref[1, :, lane], incoming, preferred_element_type=F32)).astype(BF16)

    def product(i, zb, xb):
        start = pl.multiple_of((zb * nx + xb) * rows, rows)
        return jnp.dot(xt_ref[pl.ds(start, rows), :], dy[i], preferred_element_type=F32)

    def x_copy(i, delta, p):
        return pltpu.make_async_remote_copy(
            src_ref=xsend.at[i, delta, p - 1], dst_ref=xrecv.at[i, delta, p - 1],
            send_sem=ssx.at[i, delta, p - 1], recv_sem=rsx.at[i, delta, p - 1],
            device_id={"ctx": z * nx + (x + p) % nx}, device_id_type=MESH)

    def z_copy(i, d, t):
        return pltpu.make_async_remote_copy(
            src_ref=zsend.at[i, d, t], dst_ref=zrecv.at[i, d, t],
            send_sem=ssz.at[i, d, t], recv_sem=rsz.at[i, d, t],
            device_id={"ctx": gather.ring_peer(d)}, device_id_type=MESH)

    order = []
    for k in range(1, nz // 2 + 1):
        order += [k] if k == nz - k else [k, nz - k]
    order.append(0)

    def side_partials(i):
        for delta in order:
            for p in range(1, nx):
                xsend[i, delta, p - 1] = product(i, (z + delta) % nz, (x + p) % nx).astype(BF16)
                started.append(x_copy(i, delta, p))
                started[-1].start()

    def own_partials(i):
        for delta in order:
            own[delta] = product(i, (z + delta) % nz, x)

    arrived = set()

    def reduce_step(i, d, t):
        delta = (nz - 1 - t) if d == 0 else (t + 1) % nz
        for p in range(1, nx):
            if (i, delta, p) not in arrived:
                arrived.add((i, delta, p))
                x_copy(i, delta, p).wait_recv()
        part = slice(d * half, (d + 1) * half)
        total = own[delta, part, :]
        for p in range(1, nx):
            total = total + xrecv[i, delta, p - 1, part, :].astype(F32)
        if t > 0:
            z_copy(i, d, t - 1).wait_recv()
            total = total + zrecv[i, d, t - 1].astype(F32)
        if t < nz - 1:
            zsend[i, d, t] = total.astype(BF16)
            started.append(z_copy(i, d, t))
            started[-1].start()
            return
        grad = total / tokens
        master = m_ref[i, part, :]
        first = 0.9 * m1_ref[i, part, :] + 0.1 * grad
        second = 0.95 * m2_ref[i, part, :] + 0.05 * grad * grad
        updated = master - 0.003 * (first / (jnp.sqrt(second) + 1e-08) + 0.1 * master)
        start = pl.multiple_of(me * rows + d * half, half)
        out_ref[i, pl.ds(start, half), :] = updated.astype(BF16)
        gather.send(i, d, 0)

    side_partials(0)
    key_value_grads()
    side_partials(1)
    side_partials(2)
    for i in range(4):
        if i < 3:
            own_partials(i)
        for t in range(nz):
            for d in range(2):
                if i < 3:
                    reduce_step(i, d, t)
                if i > 0 and t < nz - 1:
                    gather.ring_step(i - 1, d, t)
    for i in range(3):
        gather.wait_side(i)
    gather.finish()
    for level in range(depth):
        started += exchange(level)
    for copy in started:
        copy.wait_send()


def attend_and_update(projected, out_grad, factors, xt, master, moment_one, moment_two, nz, nx, scale, depth):
    rows, cols = master.shape[1:]
    heads, tokens = factors.shape[:2]
    size = cols // heads
    dma = pltpu.SemaphoreType.DMA
    vmem = pl.BlockSpec(memory_space=pltpu.VMEM)
    return pl.pallas_call(
        functools.partial(update_kernel, nz, nx, scale, depth),
        out_shape=(jax.ShapeDtypeStruct((tokens, cols), BF16), jax.ShapeDtypeStruct((3, xt.shape[0], cols), BF16)),
        in_specs=[vmem] * 7,
        out_specs=(vmem, vmem),
        scratch_shapes=[
            pltpu.VMEM((4, tokens, cols), F32),
            pltpu.VMEM((3, tokens, cols), BF16),
            pltpu.VMEM((heads, size, size), F32),
            pltpu.VMEM((depth, heads, size, size), F32),
            pltpu.VMEM((depth, heads, size, size), F32),
            pltpu.VMEM((depth, heads, size, size), F32),
            pltpu.VMEM((depth, depth, heads, size, size), BF16),
            pltpu.VMEM((depth, depth, heads, size, size), BF16),
            pltpu.VMEM((nz, rows, cols), F32),
            pltpu.VMEM((3, nz, nx - 1, rows, cols), BF16),
            pltpu.VMEM((3, nz, nx - 1, rows, cols), BF16),
            pltpu.VMEM((3, 2, nz - 1, rows // 2, cols), BF16),
            pltpu.VMEM((3, 2, nz - 1, rows // 2, cols), BF16),
            dma((depth,)), dma((depth,)), dma((depth,)), dma((depth,)),
            dma((3, nz, nx - 1)), dma((3, nz, nx - 1)),
            dma((3, 2, nz - 1)), dma((3, 2, nz - 1)),
            dma((3, 2, nz - 1, nx)), dma((3, 2, nz - 1, nx)),
            dma((3, 2, nz, nx - 1)), dma((3, 2, nz, nx - 1)),
        ],
        compiler_params=pltpu.CompilerParams(collective_id=1, has_side_effects=True, vmem_limit_bytes=VMEM_LIMIT),
    )(projected, out_grad, factors, xt, master, moment_one, moment_two)


def body(inputs, level_factors, out_grad, master, moment_one, moment_two):
    tokens_dev = inputs.shape[0]
    heads = level_factors.shape[0]
    head_size = out_grad.shape[1] // heads
    blocks = lax.axis_size("ctx")
    nz, nx = factor_ctx(blocks)
    depth = min(blocks.bit_length() - 1, level_factors.shape[1] - LV_IN)
    scale = 1.0 / math.sqrt(head_size * tokens_dev)
    projected, xt, factors = project(inputs, master, level_factors, nz, nx, lax.axis_size("head"))
    return attend_and_update(
        projected, out_grad, factors, xt, master, moment_one, moment_two, nz, nx, scale, depth)


def solution(mesh):
    placed = (
        P("ctx", "head"),
        P("head", None, "ctx"),
        P("ctx", "head"),
        P(None, "ctx", "head"),
        P(None, "ctx", "head"),
        P(None, "ctx", "head"),
    )
    return jax.shard_map(
        body,
        mesh=mesh,
        in_specs=placed,
        out_specs=(P("ctx", "head"), P(None, None, "head")),
        check_vma=False,
    )
```

time: 293 us -> 306 us (1.044)
  Pallas kernels: 255 us -> 295 us
  waiting for transfers between devices: 19.1 us -> 0 us
  starting transfers between devices: 3.96 us -> 0 us
  other arithmetic: 3.06 us -> 0 us
    pallas_call x4 -> x1, Pallas kernels: 174 us -> 211 us  [attend_and_update(): pl.pallas_call(functools.partial(update_kernel, nz, nx, scale, depth), ou...]
    ppermute x6 -> x0, waiting for transfers between devices: 19.1 us -> none  [from_partner(): return lax.ppermute(value, axis, pairs)]
    ppermute x6 -> x0, starting transfers between devices: 3.96 us -> none  [from_partner(): return lax.ppermute(value, axis, pairs)]
    pallas_call x1, Pallas kernels: 81.1 us -> 84.2 us  [project(): pl.pallas_call(functools.partial(project_kernel, nz, nx, nh), out_shape=(...]
    unnamed x6 -> x3, local copies, waits for them, and re-layouts: 9.33 us -> 9.92 us
  transfers between devices with their start and end apart: 6 -> 0, of which waited for: 4 -> 0; matrix products, arithmetic and copies ran while one was open for 1% -> 0% of each run, Pallas kernels for 5% -> 0%
where the time goes in v2:
time: 306 us
  Pallas kernels  295 us (96%)
  local copies, waits for them, and re-layouts  9.92 us (3%)
    pallas_call x1, Pallas kernels, attend_and_update(): pl.pallas_call(functools.partial(update_kernel, nz, nx, scale, depth), ou...  211 us
    pallas_call x1, Pallas kernels, project(): pl.pallas_call(functools.partial(project_kernel, nz, nx, nh), out_shape=(...  84.2 us
    unnamed x3, local copies, waits for them, and re-layouts  9.92 us

profile of v2, /device:TPU:4, one launch (start us, length us, event | category | flops | bytes accessed | tf_op | source)
XLA Modules:
  0.0 305.6 jit_solution(12950637603308065750)
XLA Ops:
  0.6 1.8 copy.8.f_ref
  2.4 84.2 %shard_map.77 = (bf16[3,1024,512]{2,1,0:T(8,128)(2,1)}, bf16[2048,1024]{1,0:T(8,128)(2,1)}, f32[4,1024,13]{2,1,0:T(8,128)}) custom-call(bf16[1024,512]{1,0:T(8,128)(2,1)} %x_ref.1, f32[3,256,512]{2,1,0:T(8,128)} %m_ref.3, f32[4,13,1024]{2,1,0:T(8,128)} %copy.8.f_ref), custom_call_target="tpu_custom_call" | custom-call | tf_op jit(solution)/shard_map/pallas_call | solution.py:196
  86.6 210.9 %shard_map.78 = (bf16[1024,512]{1,0:T(8,128)(2,1)}, bf16[3,2048,512]{2,1,0:T(8,128)(2,1)}) custom-call(bf16[3,1024,512]{2,1,0:T(8,128)(2,1)} %get-tuple-element.5.p_ref, bf16[1024,512]{1,0:T(8,128)(2,1)} %g_ref.1, f32[4,1024,13]{2,1,0:T(8,128)} %get-tuple-element.6.f_ref, bf16[2048,1024]{1,0:T(8,128)(2,1)} %get-tuple-element.7.xt_ref, f32[3,256,512]{2,1,0:T(8,128)} %m_ref.3, ...), custom_call_target="tpu_custom_call" | custom-call | tf_op jit(solution)/shard_map/pallas_call | solution.py:436
  297.5 2.3 copy.11
  299.8 5.9 %copy.12 = bf16[3,2048,512]{2,1,0:T(8,128)(2,1)} copy(bf16[3,2048,512]{2,1,0:T(8,128)(2,1)} %get-tuple-element.11) | data formatting | bytes 12582912

commit v3 on v2

--- a/solution.py
+++ b/solution.py
@@ -177,8 +177,10 @@
         span = pl.ds(pl.multiple_of(r * piece, piece), piece)
         xt_ref[span, :] = xs[:, span].T
 
+    gather.wait_side(0)
+    dots(0)
     ring(2)
-    for i in range(3):
+    for i in range(1, 3):
         gather.wait_side(i)
         dots(i)
     gather.finish()
@@ -271,42 +273,55 @@
     greet(ctx_peers(nz, nx) + [partner(level) for level in range(depth)])
     started = []
 
-    def exchange(level):
-        return [
-            pltpu.make_async_remote_copy(
-                src_ref=sum_out.at[level], dst_ref=sum_in.at[level], send_sem=sse.at[level], recv_sem=rse.at[level],
-                device_id=partner(level), device_id_type=MESH),
-            pltpu.make_async_remote_copy(
-                src_ref=pend_out.at[level, pl.ds(level, depth - level)],
-                dst_ref=pend_in.at[level, pl.ds(level, depth - level)],
-                send_sem=spe.at[level], recv_sem=rpe.at[level],
-                device_id=partner(level), device_id_type=MESH)]
-
-    def exchange_start(level):
-        sum_out[level] = sums[...]
+    def state_copy(level):
+        return pltpu.make_async_remote_copy(
+            src_ref=sum_out.at[level], dst_ref=sum_in.at[level], send_sem=sse.at[level], recv_sem=rse.at[level],
+            device_id=partner(level), device_id_type=MESH)
+
+    def pend_copy(level):
+        return pltpu.make_async_remote_copy(
+            src_ref=pend_out.at[level, pl.ds(level, depth - level)],
+            dst_ref=pend_in.at[level, pl.ds(level, depth - level)],
+            send_sem=spe.at[level], recv_sem=rpe.at[level],
+            device_id=partner(level), device_id_type=MESH)
+
+    def state_start(level):
+        sum_out[level] = sums[...].astype(BF16)
+        state_copy(level).start()
+
+    def state_end(level):
+        state_copy(level).wait_recv()
+        if level + 1 < depth:
+            sums[...] += sum_in[level].astype(F32)
+            state_start(level + 1)
+
+    def pend_start(level):
         pend_out[level, level:] = pend[level:].astype(BF16)
-        for copy in exchange(level):
-            copy.start()
-
-    def exchange_end(level):
-        for copy in exchange(level):
-            copy.wait_recv()
+        pend_copy(level).start()
+
+    def pend_end(level):
+        pend_copy(level).wait_recv()
         if level + 1 < depth:
-            sums[...] += sum_in[level]
             pend[level + 1:] += pend_in[level, level + 1:].astype(F32)
-            exchange_start(level + 1)
+            pend_start(level + 1)
+
+    @pl.loop(0, heads)
+    def _(h):
+        lane = pl.ds(pl.multiple_of(h * size, size), size)
+        sums[h] = dot_t(p_ref[1, :, lane], p_ref[2, :, lane])
+
+    state_start(0)
 
     @pl.loop(0, heads)
     def _(h):
         lane = pl.ds(pl.multiple_of(h * size, size), size)
         queries = p_ref[0, :, lane]
-        sums[h] = dot_t(p_ref[1, :, lane], p_ref[2, :, lane])
         grads = g_ref[:, lane].astype(F32)
         for level in range(depth):
             weighted = (f_ref[h, :, LV_IN + level:LV_IN + level + 1] * grads).astype(BF16)
             pend[level, h] = scale * dot_t(queries, weighted)
 
-    exchange_start(0)
+    pend_start(0)
 
     @pl.loop(0, heads)
     def _(h):
@@ -314,7 +329,11 @@
         for level in range(depth):
             @pl.when(h == min(level, heads - 1))
             def _():
-                exchange_end(level)
+                state_end(level)
+        for level in range(depth - 1):
+            @pl.when(h == min(level + 2, heads - 1))
+            def _():
+                pend_end(level)
 
     @pl.loop(0, heads)
     def _(h):
@@ -325,7 +344,7 @@
         for level in range(depth):
             factor = f_ref[h, :, LV_IN + level:LV_IN + level + 1]
             upper = jnp.full((size, size), (me >> level) & 1) == 1
-            bucket = jnp.where(upper, sum_in[level, h], 0.0).astype(BF16)
+            bucket = jnp.where(upper, sum_in[level, h].astype(F32), 0.0).astype(BF16)
             outer = outer + factor * jnp.dot(queries, bucket, preferred_element_type=F32)
             back = back + factor * dot_nt(grads, bucket)
         att_ref[:, lane] = (acc[0, :, lane] + scale * outer).astype(BF16)
@@ -406,6 +425,7 @@
         gather.send(i, d, 0)
 
     side_partials(0)
+    pend_end(depth - 1)
     key_value_grads()
     side_partials(1)
     side_partials(2)
@@ -422,7 +442,7 @@
         gather.wait_side(i)
     gather.finish()
     for level in range(depth):
-        started += exchange(level)
+        started += [state_copy(level), pend_copy(level)]
     for copy in started:
         copy.wait_send()
 
@@ -443,8 +463,8 @@
             pltpu.VMEM((3, tokens, cols), BF16),
             pltpu.VMEM((heads, size, size), F32),
             pltpu.VMEM((depth, heads, size, size), F32),
-            pltpu.VMEM((depth, heads, size, size), F32),
-            pltpu.VMEM((depth, heads, size, size), F32),
+            pltpu.VMEM((depth, heads, size, size), BF16),
+            pltpu.VMEM((depth, heads, size, size), BF16),
             pltpu.VMEM((depth, depth, heads, size, size), BF16),
             pltpu.VMEM((depth, depth, heads, size, size), BF16),
             pltpu.VMEM((nz, rows, cols), F32),

time: 306 us -> 284 us (0.928)
  Pallas kernels: 295 us -> 273 us
    pallas_call x1, Pallas kernels: 211 us -> 186 us  [attend_and_update(): pl.pallas_call(functools.partial(update_kernel, nz, nx, scale, depth), ou...]
where the time goes in v3:
time: 284 us; the launch traced here: 283 us
  Pallas kernels  273 us (96%)
  local copies, waits for them, and re-layouts  9.92 us (3%)
    pallas_call x1, Pallas kernels, attend_and_update(): pl.pallas_call(functools.partial(update_kernel, nz, nx, scale, depth), ou...  186 us
    pallas_call x1, Pallas kernels, project(): pl.pallas_call(functools.partial(project_kernel, nz, nx, nh), out_shape=(...  86.7 us
    unnamed x3, local copies, waits for them, and re-layouts  9.92 us

profile of v3, /device:TPU:4, one launch (start us, length us, event | category | flops | bytes accessed | tf_op | source)
XLA Modules:
  0.0 283.1 jit_solution(17819256417353549645)
XLA Ops:
  0.6 1.8 copy.8.f_ref
  2.4 86.7 %shard_map.77 = (bf16[3,1024,512]{2,1,0:T(8,128)(2,1)}, bf16[2048,1024]{1,0:T(8,128)(2,1)}, f32[4,1024,13]{2,1,0:T(8,128)}) custom-call(bf16[1024,512]{1,0:T(8,128)(2,1)} %x_ref.1, f32[3,256,512]{2,1,0:T(8,128)} %m_ref.3, f32[4,13,1024]{2,1,0:T(8,128)} %copy.8.f_ref), custom_call_target="tpu_custom_call" | custom-call | tf_op jit(solution)/shard_map/pallas_call | solution.py:198
  89.1 185.9 %shard_map.78 = (bf16[1024,512]{1,0:T(8,128)(2,1)}, bf16[3,2048,512]{2,1,0:T(8,128)(2,1)}) custom-call(bf16[3,1024,512]{2,1,0:T(8,128)(2,1)} %get-tuple-element.5.p_ref, bf16[1024,512]{1,0:T(8,128)(2,1)} %g_ref.1, f32[4,1024,13]{2,1,0:T(8,128)} %get-tuple-element.6.f_ref, bf16[2048,1024]{1,0:T(8,128)(2,1)} %get-tuple-element.7.xt_ref, f32[3,256,512]{2,1,0:T(8,128)} %m_ref.3, ...), custom_call_target="tpu_custom_call" | custom-call | tf_op jit(solution)/shard_map/pallas_call | solution.py:456
  275.0 2.3 copy.11
  277.2 5.9 %copy.12 = bf16[3,2048,512]{2,1,0:T(8,128)(2,1)} copy(bf16[3,2048,512]{2,1,0:T(8,128)(2,1)} %get-tuple-element.11) | data formatting | bytes 12582912

commit v4 on v3

--- a/solution.py
+++ b/solution.py
@@ -255,7 +255,7 @@
 
 
 def update_kernel(nz, nx, scale, depth, p_ref, g_ref, f_ref, xt_ref, m_ref, m1_ref, m2_ref, att_ref, out_ref,
-                  acc, dy, sums, pend, sum_out, sum_in, pend_out, pend_in,
+                  acc, dy, sums, pend, sum_out, sum_in, top_out, top_in, pend_out, pend_in,
                   own, xsend, xrecv, zsend, zrecv, sse, rse, spe, rpe, ssx, rsx, ssz, rsz, sz, rz, sx, rx):
     rows = m_ref.shape[1]
     half = rows // 2
@@ -274,8 +274,10 @@
     started = []
 
     def state_copy(level):
-        return pltpu.make_async_remote_copy(
-            src_ref=sum_out.at[level], dst_ref=sum_in.at[level], send_sem=sse.at[level], recv_sem=rse.at[level],
+        last = level == depth - 1
+        return pltpu.make_async_remote_copy(
+            src_ref=top_out if last else sum_out.at[level], dst_ref=top_in if last else sum_in.at[level],
+            send_sem=sse.at[level], recv_sem=rse.at[level],
             device_id=partner(level), device_id_type=MESH)
 
     def pend_copy(level):
@@ -286,13 +288,16 @@
             device_id=partner(level), device_id_type=MESH)
 
     def state_start(level):
-        sum_out[level] = sums[...].astype(BF16)
+        if level < depth - 1:
+            sum_out[level] = sums[...]
+        else:
+            top_out[...] = sums[...].astype(BF16)
         state_copy(level).start()
 
     def state_end(level):
         state_copy(level).wait_recv()
         if level + 1 < depth:
-            sums[...] += sum_in[level].astype(F32)
+            sums[...] += sum_in[level]
             state_start(level + 1)
 
     def pend_start(level):
@@ -344,7 +349,8 @@
         for level in range(depth):
             factor = f_ref[h, :, LV_IN + level:LV_IN + level + 1]
             upper = jnp.full((size, size), (me >> level) & 1) == 1
-            bucket = jnp.where(upper, sum_in[level, h].astype(F32), 0.0).astype(BF16)
+            sent = sum_in[level, h] if level < depth - 1 else top_in[h].astype(F32)
+            bucket = jnp.where(upper, sent, 0.0).astype(BF16)
             outer = outer + factor * jnp.dot(queries, bucket, preferred_element_type=F32)
             back = back + factor * dot_nt(grads, bucket)
         att_ref[:, lane] = (acc[0, :, lane] + scale * outer).astype(BF16)
@@ -463,8 +469,10 @@
             pltpu.VMEM((3, tokens, cols), BF16),
             pltpu.VMEM((heads, size, size), F32),
             pltpu.VMEM((depth, heads, size, size), F32),
-            pltpu.VMEM((depth, heads, size, size), BF16),
-            pltpu.VMEM((depth, heads, size, size), BF16),
+            pltpu.VMEM((depth, heads, size, size), F32),
+            pltpu.VMEM((depth, heads, size, size), F32),
+            pltpu.VMEM((heads, size, size), BF16),
+            pltpu.VMEM((heads, size, size), BF16),
             pltpu.VMEM((depth, depth, heads, size, size), BF16),
             pltpu.VMEM((depth, depth, heads, size, size), BF16),
             pltpu.VMEM((nz, rows, cols), F32),

time: 284 us -> 283 us (level)
  no operation moved by 1% of the time
where the time goes in v4:
time: 283 us
  Pallas kernels  272 us (96%)
  local copies, waits for them, and re-layouts  9.92 us (4%)
    pallas_call x1, Pallas kernels, attend_and_update(): pl.pallas_call(functools.partial(update_kernel, nz, nx, scale, depth), ou...  185 us
    pallas_call x1, Pallas kernels, project(): pl.pallas_call(functools.partial(project_kernel, nz, nx, nh), out_shape=(...  86.7 us
    unnamed x3, local copies, waits for them, and re-layouts  9.92 us

profile of v4, /device:TPU:4, one launch (start us, length us, event | category | flops | bytes accessed | tf_op | source)
XLA Modules:
  0.0 282.6 jit_solution(678841033693611697)
XLA Ops:
  0.6 1.8 copy.8.f_ref
  2.4 86.7 %shard_map.77 = (bf16[3,1024,512]{2,1,0:T(8,128)(2,1)}, bf16[2048,1024]{1,0:T(8,128)(2,1)}, f32[4,1024,13]{2,1,0:T(8,128)}) custom-call(bf16[1024,512]{1,0:T(8,128)(2,1)} %x_ref.1, f32[3,256,512]{2,1,0:T(8,128)} %m_ref.3, f32[4,13,1024]{2,1,0:T(8,128)} %copy.8.f_ref), custom_call_target="tpu_custom_call" | custom-call | tf_op jit(solution)/shard_map/pallas_call | solution.py:198
  89.1 185.4 %shard_map.78 = (bf16[1024,512]{1,0:T(8,128)(2,1)}, bf16[3,2048,512]{2,1,0:T(8,128)(2,1)}) custom-call(bf16[3,1024,512]{2,1,0:T(8,128)(2,1)} %get-tuple-element.5.p_ref, bf16[1024,512]{1,0:T(8,128)(2,1)} %g_ref.1, f32[4,1024,13]{2,1,0:T(8,128)} %get-tuple-element.6.f_ref, bf16[2048,1024]{1,0:T(8,128)(2,1)} %get-tuple-element.7.xt_ref, f32[3,256,512]{2,1,0:T(8,128)} %m_ref.3, ...), custom_call_target="tpu_custom_call" | custom-call | tf_op jit(solution)/shard_map/pallas_call | solution.py:462
  274.5 2.3 copy.11
  276.7 5.9 %copy.12 = bf16[3,2048,512]{2,1,0:T(8,128)(2,1)} copy(bf16[3,2048,512]{2,1,0:T(8,128)(2,1)} %get-tuple-element.11) | data formatting | bytes 12582912
